TPU v7x, 32 devices: a whole 2x2x4 slice. The times are simulated.
32 devices in a mesh: section: 2 (over core), seq: 4 (over z), head: 4 (over y, x).
Axes of the slice: x: 2, y: 2, z: 4, core: 2. Of those that a mesh axis runs over, the one named last changes fastest.
Arguments:
- tokens: bfloat16 [2, 1024, 768], P(None, 'seq'), may hold values from -12 to 12
- cotangent: bfloat16 [2, 1024, 768], P(None, 'seq'), may hold values from -6 to 6
- lengths: int32 [2], replicated, may hold values from 256 to 1024, as said below
- clusters: int32 [2, 12, 1024], P(None, 'head', 'seq'), may hold values from 0 to 99, as said below
- top_index: int32 [2, 12, 100, 32], P(None, 'head'), may hold values from 0 to 1023, as said below
- w_qkv: bfloat16 [2, 3, 768, 768], P('section', None, None, 'head'), may hold values from -1 to 1
- w_out: bfloat16 [2, 768, 768], P('section', 'head'), may hold values from -0.21875 to 0.21875
- w_in: bfloat16 [2, 768, 3072], P('section', None, 'head'), may hold values from -0.21875 to 0.21875
- w_back: bfloat16 [2, 3072, 768], P('section', 'head'), may hold values from -0.109375 to 0.109375
- gains: bfloat16 [2, 2, 768], P('section'), may hold values from 0.099609375 to 1.8984375
Outputs:
- acts: float32 [2, 2, 1024, 768], P('section', None, 'seq')
- in_grads: float32 [2, 2, 1024, 768], P('section', None, 'seq')
- grad_qkv: float32 [2, 3, 768, 768], P('section', None, 'seq', 'head')
- grad_out: float32 [2, 768, 768], P('section', 'head', 'seq')
- grad_in: float32 [2, 768, 3072], P('section', 'seq', 'head')
- grad_back: float32 [2, 3072, 768], P('section', 'head', 'seq')
- grad_gains: float32 [2, 2, 768], P('section', None, 'seq')
Inputs may be any that keep to these rules, and one draw needn't show every extreme that they name: `lengths`: one micro-batch, drawn from the seed, has length 1024. `clusters`: every cluster of every head has at least one member below its micro-batch's length. `top_index`: the 32 positions of a cluster are distinct and below its micro-batch's length. All clusters of all heads of one micro-batch name together exactly 64 distinct positions.
All inputs are finite; a program needn't handle non-finite values.
Results may differ from a plain program's by a relative error of at most 0.019.
Values may be sent and summed in bfloat16 or wider, within the bound.
No kernel may reach another device: no remote copies, remote signals or barrier semaphores. Data moves between devices by JAX's collectives and lax.ppermute only.
A program may use at most 192 MiB of HBM per device.

v0:
```python
import jax
import jax.numpy as jnp
from jax import lax
from jax.sharding import PartitionSpec as P

epsilon = 1e-05
negative = -1e30
highest = lax.Precision.HIGHEST


def from_behind(block, axis, distance):
    devices = range(lax.axis_size(axis))
    route = [(i - distance, i) for i in devices if i - distance in devices]
    return lax.ppermute(block, axis, route)


def layer_stats(values):
    centred = values - jnp.mean(values, axis=-1, keepdims=True)
    inverse = lax.rsqrt(jnp.mean(centred * centred, axis=-1, keepdims=True) + epsilon)
    return (centred * inverse, inverse)


def norm_back(grad_hat, normed, inverse):
    return inverse * (
        grad_hat
        - jnp.mean(grad_hat, axis=-1, keepdims=True)
        - normed * jnp.mean(grad_hat * normed, axis=-1, keepdims=True)
    )


def pick_entry(lookup, where_at):
    return lax.dynamic_index_in_dim(lookup, where_at, 0, keepdims=False)


def head_sum(values):
    return lax.psum(values.astype(jnp.bfloat16), "head").astype(jnp.float32)


def grad_head_sum(values):
    return lax.psum(values.astype(jnp.bfloat16), "head").astype(jnp.float32)


def split_heads(merged, head_count):
    return merged.reshape(merged.shape[0], head_count, -1).transpose(1, 0, 2)


def merge_heads(split_up):
    return split_up.transpose(1, 0, 2).reshape(split_up.shape[1], -1)


def top_local(top_index, positions):
    hits = jnp.any(top_index[..., None] == positions[None, None, None, :], axis=2)
    return hits.astype(jnp.float32)


def cluster_table(clusters, live_mask, cluster_count):
    matches = clusters[:, :, None] == jnp.arange(cluster_count, dtype=jnp.int32)[None, None, :]
    return matches.astype(jnp.float32) * live_mask[None, :, None]


def select_rows(member_bf, top_rows, tok_rows, hd_size):
    head_count, cluster_count, slot_count = (
        top_rows.shape[0],
        top_rows.shape[1],
        top_rows.shape[2],
    )
    chosen = jnp.einsum(
        "htc,hcf->htf",
        member_bf,
        top_rows.reshape(head_count, cluster_count, -1),
        preferred_element_type=jnp.float32,
    )
    return chosen.astype(jnp.bfloat16).reshape(head_count, tok_rows, slot_count, 2 * hd_size)


def member_weights(queries, chosen, hd_size, inv_root):
    logits = (
        jnp.einsum(
            "htd,htjd->htj", queries, chosen[..., :hd_size], preferred_element_type=jnp.float32
        )
        * inv_root
    )
    exponent = jnp.exp(logits - jnp.max(logits, axis=-1, keepdims=True))
    member_prob = exponent / jnp.sum(exponent, axis=-1, keepdims=True)
    return (member_prob, member_prob.astype(jnp.bfloat16))


def local_pieces(projected, clusters, length, offset, cluster_count):
    head_count = clusters.shape[0]
    tok_rows = projected.shape[0]
    queries = split_heads(projected[:, 0], head_count)
    key_local = split_heads(projected[:, 1], head_count)
    value_local = split_heads(projected[:, 2], head_count)
    positions = offset + jnp.arange(tok_rows, dtype=jnp.int32)
    live_mask = (positions < length).astype(jnp.float32)
    member_table = cluster_table(clusters, live_mask, cluster_count)
    return (queries, key_local, value_local, positions, live_mask, member_table)


def forward_layer(source, weights, clusters, top_index, length, offset, total_rows):
    w_qkv, w_out, w_in, w_back, gains = weights
    head_count = clusters.shape[0]
    cluster_count = top_index.shape[1]
    tok_rows = source.shape[0]
    hd_size = w_qkv.shape[2] // head_count
    inv_root = hd_size ** (-0.5)
    hat_one, inv_one = layer_stats(source)
    normed_one = (hat_one * gains[0]).astype(jnp.bfloat16)
    projected = jnp.einsum(
        "td,ide->tie", normed_one, w_qkv, preferred_element_type=jnp.float32
    ).astype(jnp.bfloat16)
    queries, key_local, value_local, positions, live_mask, member_table = local_pieces(
        projected, clusters, length, offset, cluster_count
    )
    paired = jnp.concatenate([key_local, value_local], axis=-1)
    member_bf = member_table.astype(jnp.bfloat16)
    cluster_sums = jnp.einsum(
        "htc,htd->hcd", member_bf, queries, preferred_element_type=jnp.float32
    )
    counts = jnp.sum(member_table, axis=1)
    cluster_sums, counts = (
        lax.psum(cluster_sums.astype(jnp.bfloat16), "seq").astype(jnp.float32),
        lax.psum(counts.astype(jnp.bfloat16), "seq").astype(jnp.float32),
    )
    centre = (cluster_sums / counts[..., None]).astype(jnp.bfloat16)
    everyone = lax.all_gather(paired, "seq", axis=1, tiled=True)
    scores = (
        jnp.einsum(
            "hcd,htd->hct", centre, everyone[..., :hd_size], preferred_element_type=jnp.float32
        )
        * inv_root
    )
    all_pos = jnp.arange(total_rows, dtype=jnp.int32)
    live_all = (all_pos < length).astype(jnp.float32)
    head_ids = jnp.arange(head_count, dtype=jnp.int32)[:, None, None]
    clus_ids = jnp.arange(cluster_count, dtype=jnp.int32)[None, :, None]
    in_top = (
        jnp.zeros((head_count, cluster_count, total_rows), jnp.float32)
        .at[head_ids, clus_ids, top_index]
        .set(1.0)
    )
    peak_score = jnp.max(jnp.where(live_all[None, None, :] > 0, scores, negative), axis=2)
    weighted = jnp.exp(scores - peak_score[..., None]) * live_all[None, None, :]
    carried = jnp.einsum(
        "hct,htd->hcd",
        (weighted * (1.0 - in_top)).astype(jnp.bfloat16),
        everyone[..., hd_size:],
        preferred_element_type=jnp.float32,
    )
    total_mass = jnp.sum(weighted, axis=2)
    top_mass = jnp.sum(weighted * in_top, axis=2)
    top_rows = jax.vmap(lambda lookup, where_at: lookup[where_at])(everyone, top_index)
    chosen = select_rows(member_bf, top_rows, tok_rows, hd_size)
    member_prob, prob_bf = member_weights(queries, chosen, hd_size, inv_root)
    top_out = jnp.einsum(
        "htj,htjd->htd", prob_bf, chosen[..., hd_size:], preferred_element_type=jnp.float32
    )
    remote = carried / total_mass[..., None]
    top_share = top_mass / total_mass
    remote_rows = jnp.einsum("htc,hcd->htd", member_table, remote, precision=highest)
    share_rows = jnp.einsum("htc,hc->ht", member_table, top_share, precision=highest)
    attention = live_mask[None, :, None] * (share_rows[..., None] * top_out + remote_rows)
    attention_bf = merge_heads(attention).astype(jnp.bfloat16)
    middle = source + head_sum(jnp.dot(attention_bf, w_out, preferred_element_type=jnp.float32))
    hat_two, inv_two = layer_stats(middle)
    normed_two = (hat_two * gains[1]).astype(jnp.bfloat16)
    hidden = jnp.dot(normed_two, w_in, preferred_element_type=jnp.float32)
    active = jax.nn.gelu(hidden).astype(jnp.bfloat16)
    result = middle + head_sum(jnp.dot(active, w_back, preferred_element_type=jnp.float32))
    saved_state = (
        source,
        middle,
        normed_one,
        projected,
        centre,
        counts,
        peak_score,
        total_mass,
        top_mass,
        carried,
        top_rows,
        attention_bf,
        normed_two,
        hidden,
        active,
    )
    return (result, saved_state)


def backward_layer(grad_out, saved_state, weights, clusters, top_index, length, offset, total_rows):
    (
        source,
        middle,
        normed_one,
        projected,
        centre,
        counts,
        peak_score,
        total_mass,
        top_mass,
        carried,
        top_rows,
        attention_bf,
        normed_two,
        hidden,
        active,
    ) = saved_state
    w_qkv, w_out, w_in, w_back, gains = weights
    head_count = clusters.shape[0]
    cluster_count = top_index.shape[1]
    tok_rows = source.shape[0]
    hd_size = w_qkv.shape[2] // head_count
    inv_root = hd_size ** (-0.5)
    grad_out_bf = grad_out.astype(jnp.bfloat16)
    grad_wback = jnp.einsum("tf,td->fd", active, grad_out_bf, preferred_element_type=jnp.float32)
    grad_active = jnp.einsum("td,fd->tf", grad_out_bf, w_back, preferred_element_type=jnp.float32)
    gelu_value, gelu_pull = jax.vjp(jax.nn.gelu, hidden)
    grad_hidden = gelu_pull(grad_active)[0].astype(jnp.bfloat16)
    grad_win = jnp.einsum("td,tf->df", normed_two, grad_hidden, preferred_element_type=jnp.float32)
    grad_norm_two = grad_head_sum(
        jnp.einsum("tf,df->td", grad_hidden, w_in, preferred_element_type=jnp.float32)
    )
    hat_two, inv_two = layer_stats(middle)
    gain_two = jnp.sum(grad_norm_two * hat_two, axis=0)
    grad_middle = grad_out + norm_back(grad_norm_two * gains[1], hat_two, inv_two)
    grad_middle_bf = grad_middle.astype(jnp.bfloat16)
    grad_wout = jnp.einsum(
        "te,td->ed", attention_bf, grad_middle_bf, preferred_element_type=jnp.float32
    )
    grad_att = split_heads(
        jnp.einsum("td,ed->te", grad_middle_bf, w_out, preferred_element_type=jnp.float32).astype(
            jnp.bfloat16
        ),
        head_count,
    )
    queries, key_local, value_local, positions, live_mask, member_table = local_pieces(
        projected, clusters, length, offset, cluster_count
    )
    member_bf = member_table.astype(jnp.bfloat16)
    chosen = select_rows(member_bf, top_rows, tok_rows, hd_size)
    member_prob, prob_bf = member_weights(queries, chosen, hd_size, inv_root)
    top_share = top_mass / total_mass
    share_rows = jnp.einsum("htc,hc->ht", member_table, top_share, precision=highest)
    grad_top = grad_att * live_mask[None, :, None].astype(jnp.bfloat16)
    raw_prob = jnp.einsum(
        "htd,htjd->htj", grad_top, chosen[..., hd_size:], preferred_element_type=jnp.float32
    )
    top_dot = jnp.sum(prob_bf.astype(jnp.float32) * raw_prob, axis=-1)
    grad_prob = raw_prob * share_rows[..., None]
    grad_vtop = (
        jnp.einsum("htj,htd->htjd", prob_bf, grad_top, preferred_element_type=jnp.float32)
        * share_rows[:, :, None, None]
    )
    grad_logit = (
        member_prob * (grad_prob - jnp.sum(member_prob * grad_prob, axis=-1, keepdims=True))
    ).astype(jnp.bfloat16)
    grad_query = inv_root * jnp.einsum(
        "htj,htjd->htd", grad_logit, chosen[..., :hd_size], preferred_element_type=jnp.float32
    )
    grad_ktop = inv_root * jnp.einsum(
        "htj,htd->htjd", grad_logit, queries, preferred_element_type=jnp.float32
    )
    slot_grads = jnp.concatenate([grad_ktop, grad_vtop], axis=-1).reshape(head_count, tok_rows, -1)
    per_slot = jnp.einsum("htc,htf->hcf", member_table, slot_grads, precision=highest).reshape(
        head_count, -1, 2 * hd_size
    )
    head_ids = jnp.arange(head_count, dtype=jnp.int32)[:, None]
    flat_index = top_index.reshape(head_count, -1)
    dense_grad = (
        jnp.zeros((head_count, total_rows, 2 * hd_size), jnp.float32)
        .at[head_ids, flat_index]
        .add(per_slot)
    )
    returned = lax.psum_scatter(
        dense_grad.astype(jnp.bfloat16), "seq", scatter_dimension=1, tiled=True
    ).astype(jnp.float32)
    remote_part = jnp.einsum(
        "htc,htd->hcd", member_bf, grad_top, preferred_element_type=jnp.float32
    )
    share_part = jnp.einsum("htc,ht->hc", member_table, top_dot, precision=highest)
    grad_remote, grad_share = (
        lax.psum(remote_part.astype(jnp.bfloat16), "seq").astype(jnp.float32),
        lax.psum(share_part.astype(jnp.bfloat16), "seq").astype(jnp.float32),
    )
    grad_carried = (grad_remote / total_mass[..., None]).astype(jnp.bfloat16)
    grad_topmass = grad_share / total_mass
    grad_mass = -(jnp.sum(grad_remote * carried, axis=-1) + grad_share * top_mass) / (
        total_mass * total_mass
    )
    scores = (
        jnp.einsum("hcd,htd->hct", centre, key_local, preferred_element_type=jnp.float32) * inv_root
    )
    weighted = jnp.exp(scores - peak_score[..., None]) * live_mask[None, None, :]
    in_top = top_local(top_index, positions)
    grad_weighted = (
        (1.0 - in_top)
        * jnp.einsum("hcd,htd->hct", grad_carried, value_local, preferred_element_type=jnp.float32)
        + in_top * grad_topmass[..., None]
        + grad_mass[..., None]
    )
    grad_scores = (grad_weighted * weighted).astype(jnp.bfloat16)
    grad_centre = lax.psum(
        (
            inv_root
            * jnp.einsum("hct,htd->hcd", grad_scores, key_local, preferred_element_type=jnp.float32)
        ).astype(jnp.bfloat16),
        "seq",
    ).astype(jnp.float32)
    grad_key = (
        inv_root
        * jnp.einsum("hct,hcd->htd", grad_scores, centre, preferred_element_type=jnp.float32)
        + returned[..., :hd_size]
    )
    grad_value = (
        jnp.einsum(
            "hct,hcd->htd",
            (weighted * (1.0 - in_top)).astype(jnp.bfloat16),
            grad_carried,
            preferred_element_type=jnp.float32,
        )
        + returned[..., hd_size:]
    )
    grad_query = grad_query + jnp.einsum(
        "htc,hcd->htd", member_table, grad_centre / counts[..., None], precision=highest
    )
    grad_qkv = jnp.stack(
        [merge_heads(grad_query), merge_heads(grad_key), merge_heads(grad_value)], axis=1
    ).astype(jnp.bfloat16)
    grad_wqkv = jnp.einsum("td,tie->ide", normed_one, grad_qkv, preferred_element_type=jnp.float32)
    grad_norm_one = grad_head_sum(
        jnp.einsum("tie,ide->td", grad_qkv, w_qkv, preferred_element_type=jnp.float32)
    )
    hat_one, inv_one = layer_stats(source)
    gain_one = jnp.sum(grad_norm_one * hat_one, axis=0)
    grad_source = grad_middle + norm_back(grad_norm_one * gains[0], hat_one, inv_one)
    return (
        grad_source,
        (grad_wqkv, grad_wout, grad_win, grad_wback, jnp.stack([gain_one, gain_two])),
    )


def shards(tokens, cotangent, lengths, clusters, top_index, w_qkv, w_out, w_in, w_back, gains):
    section_at = lax.axis_index("section")
    sections = lax.axis_size("section")
    micro_count = tokens.shape[0]
    tok_rows = tokens.shape[1]
    model_dim = tokens.shape[2]
    offset = lax.axis_index("seq") * tok_rows
    total_rows = lax.axis_size("seq") * tok_rows
    weights = (w_qkv[0], w_out[0], w_in[0], w_back[0], gains[0].astype(jnp.float32))
    moments = micro_count + sections - 1
    slot_ids = jnp.arange(micro_count, dtype=jnp.int32)
    arriving = jnp.zeros((tok_rows, model_dim), jnp.float32)
    outputs = jnp.zeros((micro_count, tok_rows, model_dim), jnp.float32)
    kept_list = []
    for moment in range(moments):
        batch_at = moment - section_at
        clipped = jnp.clip(batch_at, 0, micro_count - 1)
        first_in = pick_entry(tokens, min(moment, micro_count - 1)).astype(jnp.float32)
        source = jnp.where(section_at == 0, first_in, arriving)
        result, saved_state = forward_layer(
            source,
            weights,
            pick_entry(clusters, clipped),
            pick_entry(top_index, clipped),
            pick_entry(lengths, clipped),
            offset,
            total_rows,
        )
        outputs = jnp.where((slot_ids == batch_at)[:, None, None], result[None], outputs)
        kept_list.append(saved_state)
        if moment < moments - 1:
            arriving = from_behind(result.astype(jnp.bfloat16), "section", 1).astype(result.dtype)
    stored = jax.tree.map(lambda *pieces: jnp.stack(pieces), *kept_list)
    returning = jnp.zeros((tok_rows, model_dim), jnp.float32)
    in_grads = jnp.zeros((micro_count, tok_rows, model_dim), jnp.float32)
    totals = None
    for moment in range(moments):
        batch_at = moment - (sections - 1 - section_at)
        clipped = jnp.clip(batch_at, 0, micro_count - 1)
        live_step = ((batch_at >= 0) & (batch_at < micro_count)).astype(jnp.float32)
        from_cot = pick_entry(cotangent, clipped).astype(jnp.float32)
        seed_grad = jnp.where(section_at == sections - 1, from_cot, returning) * live_step
        tick_at = jnp.clip(moment - sections + 1 + 2 * section_at, 0, moments - 1)
        saved_state = jax.tree.map(lambda piece: pick_entry(piece, tick_at), stored)
        grad_source, grads = backward_layer(
            seed_grad,
            saved_state,
            weights,
            pick_entry(clusters, clipped),
            pick_entry(top_index, clipped),
            pick_entry(lengths, clipped),
            offset,
            total_rows,
        )
        in_grads = jnp.where((slot_ids == batch_at)[:, None, None], grad_source[None], in_grads)
        totals = grads if totals is None else jax.tree.map(jnp.add, totals, grads)
        if moment < moments - 1:
            returning = from_behind(grad_source.astype(jnp.bfloat16), "section", -1).astype(
                grad_source.dtype
            )
    grad_wqkv, grad_wout, grad_win, grad_wback, grad_gain = totals
    summed = (
        lax.psum_scatter(
            grad_wqkv.astype(jnp.bfloat16), "seq", scatter_dimension=1, tiled=True
        ).astype(jnp.float32),
        lax.psum_scatter(
            grad_wout.astype(jnp.bfloat16), "seq", scatter_dimension=1, tiled=True
        ).astype(jnp.float32),
        lax.psum_scatter(
            grad_win.astype(jnp.bfloat16), "seq", scatter_dimension=0, tiled=True
        ).astype(jnp.float32),
        lax.psum_scatter(
            grad_wback.astype(jnp.bfloat16), "seq", scatter_dimension=1, tiled=True
        ).astype(jnp.float32),
        lax.psum_scatter(
            grad_gain.astype(jnp.bfloat16), "seq", scatter_dimension=1, tiled=True
        ).astype(jnp.float32),
    )
    return (
        outputs[None],
        in_grads[None],
        summed[0][None],
        summed[1][None],
        summed[2][None],
        summed[3][None],
        summed[4][None],
    )


def solution(mesh):
    placed = (
        P(None, "seq", None),
        P(None, "seq", None),
        P(),
        P(None, "head", "seq"),
        P(None, "head", None, None),
        P("section", None, None, "head"),
        P("section", "head", None),
        P("section", None, "head"),
        P("section", "head", None),
        P("section", None, None),
    )
    return jax.shard_map(
        shards,
        mesh=mesh,
        in_specs=placed,
        out_specs=(
            P("section", None, "seq", None),
            P("section", None, "seq", None),
            P("section", None, "seq", "head"),
            P("section", "head", "seq"),
            P("section", "seq", "head"),
            P("section", "head", "seq"),
            P("section", None, "seq"),
        ),
        check_vma=False,
    )
```

profile of v0, /device:TPU:0, one launch (start us, length us, event | category | flops | bytes accessed | tf_op | source)
XLA Modules:
  0.0 1939.7 jit_solution(14758650649099269156)
XLA Ops:
  17.5 22.2 %all-reduce.6 = (bf16[3,100,64]{1,2,0:T(8,128)(2,1)}, bf16[3,100]{1,0:T(4,128)(2,1)S(1)}) all-reduce(bf16[3,100,64]{1,2,0:T(8,128)(2,1)S(1)} %convolution_convert_fusion.23, bf16[3,100]{1,0:T(4,128)(2,1)S(1)} %select_reduce_fusion.5), channel_id=1, replica_groups=mesh['section'=2,'seq'=4,'head'=4] {'seq'}, use_global_device_ids=true, to_apply=%region_2.3 | all-reduce | flops 19500 | bytes 78000 | tf_op jit(solution)/shard_map/psum | solution.py:122
  40.3 16.4 all_gather.9
  59.2 46.6 %scatter_custom_fusion = f32[307200]{0:T(1024)} fusion(s32[9600]{0:T(1024)S(1)} %reshape.846, f32[9600]{0:T(1024)S(1)} %broadcast.930, f32[]{:T(128)} %constant.277.clone.1), kind=kCustom, calls=%fused_computation.478 | custom fusion | bytes 1228804
  110.7 71.6 %gather_fusion = bf16[9600,128]{1,0:T(8,128)(2,1)} fusion(bf16[3,1024,128]{2,1,0:T(8,128)(2,1)S(1)} %copy.95, s32[9600]{0:T(1024)S(1)} %reshape.828), kind=kCustom, calls=%fused_computation | custom fusion | bytes 4992000 | tf_op jit(solution)/shard_map/vmap()/gather | solution.py:152
  195.5 6.1 fusion.25
  219.8 32.2 %all-reduce.19.cloned.1.call-done = bf16[256,768]{1,0:T(8,128)(2,1)} async-done(((bf16[256,768]{1,0:T(8,128)(2,1)}), bf16[256,768]{1,0:T(8,128)(2,1)}) %all-reduce.19.cloned.1.call-update) | async-done | bytes 393232 | tf_op jit(solution)/shard_map/psum | solution.py:36
  261.2 42.8 %all-reduce.21.cloned.1.call-done = bf16[256,768]{1,0:T(8,128)(2,1)} async-done(((bf16[256,768]{1,0:T(8,128)(2,1)}), bf16[256,768]{1,0:T(8,128)(2,1)}) %all-reduce.21.cloned.1.call-update) | async-done | bytes 393232 | tf_op jit(solution)/shard_map/psum | solution.py:36
  308.4 46.6 %scatter_custom_fusion.1 = f32[307200]{0:T(1024)} fusion(s32[9600]{0:T(1024)S(1)} %reshape.852, f32[9600]{0:T(1024)} %copy-done.125, f32[]{:T(128)} %constant.277.clone.1), kind=kCustom, calls=%fused_computation.476 | custom fusion | bytes 1229312
  358.9 46.4 %scatter_custom_fusion.2 = f32[307200]{0:T(1024)} fusion(s32[9600]{0:T(1024)} %reshape.858, f32[9600]{0:T(1024)} %copy-done.125, f32[]{:T(128)} %constant.277.clone.1), kind=kCustom, calls=%fused_computation.474 | custom fusion | bytes 1229312
  422.4 19.6 %all_gather.10 = bf16[3,1024,128]{1,2,0:T(8,128)(2,1)S(1)} all-gather(bf16[3,256,128]{1,2,0:T(8,128)(2,1)S(1)} %pad_maximum_fusion.17), channel_id=1, replica_groups=mesh['section'=2,'seq'=4,'head'=4] {'seq'}, dimensions={1}, use_global_device_ids=true | all-gather | bytes 983040 | tf_op jit(solution)/shard_map/all_gather | solution.py:126
  442.9 19.2 all-reduce.5
  473.9 71.7 %gather_fusion.1 = bf16[9600,128]{1,0:T(8,128)(2,1)} fusion(bf16[3,1024,128]{2,1,0:T(8,128)(2,1)S(1)} %copy.98, s32[9600]{0:T(1024)S(1)} %reshape.834), kind=kCustom, calls=%fused_computation.1 | custom fusion | bytes 4992000 | tf_op jit(solution)/shard_map/vmap()/gather | solution.py:152
  558.8 6.9 fusion.23
  567.0 5.5 fusion.35
  577.1 11.6 compare_reduce_fusion
  588.6 29.6 %all-reduce.23.cloned.1.call-done = bf16[256,768]{1,0:T(8,128)(2,1)} async-done(((bf16[256,768]{1,0:T(8,128)(2,1)}), bf16[256,768]{1,0:T(8,128)(2,1)}) %all-reduce.23.cloned.1.call-update) | async-done | bytes 393232 | tf_op jit(solution)/shard_map/psum | solution.py:36
  626.9 41.3 %all-reduce.25.cloned.1.call-done = bf16[256,768]{1,0:T(8,128)(2,1)} async-done(((bf16[256,768]{1,0:T(8,128)(2,1)}), bf16[256,768]{1,0:T(8,128)(2,1)}) %all-reduce.25.cloned.1.call-update) | async-done | bytes 393232 | tf_op jit(solution)/shard_map/psum | solution.py:36
  676.5 19.9 %all-reduce.4 = (bf16[3,100,64]{1,2,0:T(8,128)(2,1)S(1)}, bf16[3,100]{1,0:T(4,128)(2,1)S(1)}) all-reduce(bf16[3,100,64]{1,2,0:T(8,128)(2,1)S(1)} %convolution_convert_fusion.21, bf16[3,100]{1,0:T(4,128)(2,1)S(1)} %copy-done.186), channel_id=1, replica_groups=mesh['section'=2,'seq'=4,'head'=4] {'seq'}, use_global_device_ids=true, to_apply=%region_32.33 | all-reduce | flops 19500 | bytes 78000 | tf_op jit(solution)/shard_map/psum | solution.py:122
  696.4 16.7 all_gather.11
  720.2 71.9 %gather_fusion.2 = bf16[9600,128]{1,0:T(8,128)(2,1)} fusion(bf16[3,1024,128]{2,1,0:T(8,128)(2,1)S(1)} %copy.101, s32[9600]{0:T(1024)S(1)} %reshape.840), kind=kCustom, calls=%fused_computation.2 | custom fusion | bytes 4992000 | tf_op jit(solution)/shard_map/vmap()/gather | solution.py:152
  842.0 6.1 fusion.21
  888.1 7.0 fusion.699
  909.8 41.7 %all-reduce.29.cloned.1.call-done = bf16[256,768]{1,0:T(8,128)(2,1)} async-done(((bf16[256,768]{1,0:T(8,128)(2,1)}), bf16[256,768]{1,0:T(8,128)(2,1)}) %all-reduce.29.cloned.1.call-update) | async-done | bytes 393232 | tf_op jit(solution)/shard_map/psum | solution.py:40
  960.5 7.1 fusion.19
  972.1 21.2 %all-reduce.3 = (bf16[3,100,64]{1,2,0:T(8,128)(2,1)}, bf16[3,100]{1,0:T(4,128)(2,1)}) all-reduce(bf16[3,100,64]{1,2,0:T(8,128)(2,1)} %convolution_convert_fusion.20, bf16[3,100]{1,0:T(4,128)(2,1)} %bitcast.993), channel_id=1, replica_groups=mesh['section'=2,'seq'=4,'head'=4] {'seq'}, use_global_device_ids=true, to_apply=%region_56.57 | all-reduce | flops 19500 | bytes 78000 | tf_op jit(solution)/shard_map/psum | solution.py:282
  1000.3 5.9 fusion.721
  1015.7 6.3 pad_maximum_fusion
  1022.0 13.8 reshape.779
  1035.8 11.3 fusion.285
  1047.1 5.9 reshape.866
  1052.9 53.8 %scatter_custom_fusion.3 = f32[3072,128]{1,0:T(8,128)} fusion(s32[9600]{0:T(1024)} %reshape.864, f32[9600,128]{1,0:T(8,128)} %reshape.866, f32[]{:T(128)} %constant.277.clone.1), kind=kCustom, calls=%fused_computation.391 | custom fusion | flops 1228800 | bytes 1573376
  1112.9 5.4 fusion.31
  1123.9 17.8 psum.204
  1150.1 7.1 fusion.697
  1157.1 35.8 %all-reduce.31.cloned.1.call-done = bf16[256,768]{1,0:T(8,128)(2,1)} async-done(((bf16[256,768]{1,0:T(8,128)(2,1)}), bf16[256,768]{1,0:T(8,128)(2,1)}) %all-reduce.31.cloned.1.call-update) | async-done | bytes 393232 | tf_op jit(solution)/shard_map/psum | solution.py:40
  1198.7 7.0 fusion.695
  1212.3 42.5 %all-reduce.33.cloned.1.call-done = bf16[256,768]{1,0:T(8,128)(2,1)} async-done(((bf16[256,768]{1,0:T(8,128)(2,1)}), bf16[256,768]{1,0:T(8,128)(2,1)}) %all-reduce.33.cloned.1.call-update) | async-done | bytes 393232 | tf_op jit(solution)/shard_map/psum | solution.py:40
  1263.9 7.1 fusion.17
  1275.6 21.2 %all-reduce.2 = (bf16[3,100,64]{1,2,0:T(8,128)(2,1)}, bf16[3,100]{1,0:T(4,128)(2,1)}) all-reduce(bf16[3,100,64]{1,2,0:T(8,128)(2,1)} %convolution_convert_fusion.19, bf16[3,100]{1,0:T(4,128)(2,1)} %bitcast.994), channel_id=1, replica_groups=mesh['section'=2,'seq'=4,'head'=4] {'seq'}, use_global_device_ids=true, to_apply=%region_77.78 | all-reduce | flops 19500 | bytes 78000 | tf_op jit(solution)/shard_map/psum | solution.py:282
  1303.7 6.0 fusion.724
  1319.1 6.3 pad_maximum_fusion.1
  1325.5 13.8 reshape.785
  1339.2 11.3 fusion.278
  1350.5 5.9 reshape.872
  1356.4 53.8 %scatter_custom_fusion.4 = f32[3072,128]{1,0:T(8,128)} fusion(s32[9600]{0:T(1024)} %reshape.870, f32[9600,128]{1,0:T(8,128)} %reshape.872, f32[]{:T(128)} %constant.277.clone.1), kind=kCustom, calls=%fused_computation.389 | custom fusion | flops 1228800 | bytes 1573376
  1417.0 5.4 fusion.29
  1428.0 18.0 psum.209
  1456.9 39.9 %all-reduce.35.cloned.1.call-done = bf16[256,768]{1,0:T(8,128)(2,1)} async-done(((bf16[256,768]{1,0:T(8,128)(2,1)}), bf16[256,768]{1,0:T(8,128)(2,1)}) %all-reduce.35.cloned.1.call-update) | async-done | bytes 393232 | tf_op jit(solution)/shard_map/psum | solution.py:40
  1512.6 41.4 %all-reduce.37.cloned.1.call-done = bf16[256,768]{1,0:T(8,128)(2,1)} async-done(((bf16[256,768]{1,0:T(8,128)(2,1)}), bf16[256,768]{1,0:T(8,128)(2,1)}) %all-reduce.37.cloned.1.call-update) | async-done | bytes 393232 | tf_op jit(solution)/shard_map/psum | solution.py:40
  1562.8 7.1 fusion.15
  1574.4 21.0 %all-reduce.1 = (bf16[3,100,64]{1,2,0:T(8,128)(2,1)}, bf16[3,100]{1,0:T(4,128)(2,1)}) all-reduce(bf16[3,100,64]{1,2,0:T(8,128)(2,1)} %convolution_convert_fusion.18, bf16[3,100]{1,0:T(4,128)(2,1)} %bitcast.995), channel_id=1, replica_groups=mesh['section'=2,'seq'=4,'head'=4] {'seq'}, use_global_device_ids=true, to_apply=%region_98.99 | all-reduce | flops 19500 | bytes 78000 | tf_op jit(solution)/shard_map/psum | solution.py:282
  1601.2 5.9 fusion.727
  1616.6 6.3 pad_maximum_fusion.2
  1622.9 13.8 reshape.791
  1636.7 11.3 fusion.271
  1648.0 5.9 reshape.878
  1653.9 53.8 %scatter_custom_fusion.5 = f32[3072,128]{1,0:T(8,128)} fusion(s32[9600]{0:T(1024)} %reshape.876, f32[9600,128]{1,0:T(8,128)} %reshape.878, f32[]{:T(128)} %constant.277.clone.1), kind=kCustom, calls=%fused_computation.387 | custom fusion | flops 1228800 | bytes 1573376
  1716.3 5.3 fusion.27
  1727.1 17.2 psum.214
  1773.7 26.8 %all-reduce.39.cloned.1.call-done = (bf16[256,768]{1,0:T(8,128)(2,1)}, bf16[256,768]{1,0:T(8,128)(2,1)}) async-done(((bf16[256,768]{1,0:T(8,128)(2,1)}, bf16[256,768]{1,0:T(8,128)(2,1)}), (bf16[256,768]{1,0:T(8,128)(2,1)}, bf16[256,768]{1,0:T(8,128)(2,1)})) %all-reduce.39.cloned.1.call-update) | async-done | bytes 786448 | tf_op jit(solution)/shard_map/psum | solution.py:36
  1828.0 25.6 %reduce-scatter.23.cloned.1.call-done = bf16[768,192]{0,1:T(8,128)(2,1)} async-done(((bf16[768,768]{0,1:T(8,128)(2,1)}), bf16[768,192]{0,1:T(8,128)(2,1)}) %reduce-scatter.23.cloned.1.call-update) | async-done | bytes 294928 | tf_op jit(solution)/shard_map/reduce_scatter | solution.py:413
  1861.4 13.0 reduce-scatter.29.cloned.1.call-done
  1875.9 25.2 %reduce-scatter.25.cloned.1.call-done = bf16[192,576]{1,0:T(8,128)(2,1)} async-done(((bf16[768,576]{1,0:T(8,128)(2,1)}), bf16[192,576]{1,0:T(8,128)(2,1)}) %reduce-scatter.25.cloned.1.call-update) | async-done | bytes 221200
  1903.6 27.6 %reduce-scatter.21.cloned.1.call-done = bf16[192,768]{1,0:T(8,128)(2,1)} async-done(((bf16[768,768]{1,0:T(8,128)(2,1)}), bf16[192,768]{1,0:T(8,128)(2,1)}) %reduce-scatter.21.cloned.1.call-update) | async-done | bytes 294928 | tf_op jit(solution)/shard_map/reduce_scatter | solution.py:410
  (829 shorter events, 486.4 us)
Async XLA Ops:
  7.2 251.2 %copy-start = (bf16[1,768,768]{2,1,0:T(8,128)(2,1)S(1)}, bf16[1,768,768]{2,1,0:T(8,128)(2,1)}, u32[]{:S(2)}) copy-start(bf16[1,768,768]{2,1,0:T(8,128)(2,1)} %param.18) | copy-start | bytes 3538948
  7.2 244.8 %all-reduce.19.cloned.1.call-start = ((), (), s32[]{:S(2)}) async-start(), calls=%async_computation.8 | async-start | bytes 786432 | tf_op jit(solution)/shard_map/psum | solution.py:36
  12.6 44.2 %copy-start.75 = (s32[2,3,100,32]{2,3,1,0:T(8,128)S(1)}, s32[2,3,100,32]{2,3,1,0:T(8,128)}, u32[]{:S(2)}) copy-start(s32[2,3,100,32]{2,3,1,0:T(8,128)} %param.14) | copy-start | bytes 230404
  12.6 44.9 %copy-start.195 = (s32[3]{0:T(128)S(1)}, s32[3]{0:T(128)}, u32[]{:S(2)}) copy-start(s32[3]{0:T(128)} %constant.303) | copy-start | bytes 40
  13.0 45.2 %copy-start.194 = (s32[3]{0:T(128)S(1)}, s32[3]{0:T(128)}, u32[]{:S(2)}) copy-start(s32[3]{0:T(128)} %constant.306) | copy-start | bytes 40
  13.9 45.0 %copy-start.96 = (bf16[256,1,192]{0,2,1:T(8,128)(2,1)}, bf16[256,1,192]{0,2,1:T(8,128)(2,1)S(1)}, u32[]{:S(2)}) copy-start(bf16[256,1,192]{0,2,1:T(8,128)(2,1)S(1)} %get-tuple-element.169) | copy-start | bytes 294916
  16.5 40.9 %copy-start.164 = (f32[256]{0:T(256)}, f32[256]{0:T(256)S(1)}, u32[]{:S(2)}) copy-start(f32[256]{0:T(256)S(1)} %compare_convert_fusion.5) | copy-start | bytes 3076
  59.2 49.4 %copy-start.125 = (f32[9600]{0:T(1024)}, f32[9600]{0:T(1024)S(1)}, u32[]{:S(2)}) copy-start(f32[9600]{0:T(1024)S(1)} %broadcast.930) | copy-start | bytes 115204
  109.7 97.3 %copy-start.100 = (f32[3,100,64]{1,2,0:T(8,128)}, f32[3,100,64]{1,2,0:T(8,128)S(1)}, u32[]{:S(2)}) copy-start(f32[3,100,64]{1,2,0:T(8,128)S(1)} %fusion.294) | copy-start | bytes 230404
  207.0 44.9 %copy-start.2 = (bf16[2,256,768]{2,1,0:T(8,128)(2,1)S(1)}, bf16[2,256,768]{2,1,0:T(8,128)(2,1)}, u32[]{:S(2)}) copy-start(bf16[2,256,768]{2,1,0:T(8,128)(2,1)} %param.10) | copy-start | bytes 2359300
  208.5 95.5 %all-reduce.21.cloned.1.call-start = ((), (), s32[]{:S(2)}) async-start(), calls=%async_computation.9 | async-start | bytes 786432 | tf_op jit(solution)/shard_map/psum | solution.py:36
  209.1 46.4 %copy-start.83 = (s32[1,3,100,32]{2,3,1,0:T(8,128)}, s32[1,3,100,32]{2,3,1,0:T(8,128)S(1)}, u32[]{:S(2)}) copy-start(s32[1,3,100,32]{2,3,1,0:T(8,128)S(1)} %get-tuple-element.179) | copy-start | bytes 115204
  209.2 46.4 %copy-start.84 = (s32[1,3,100,32]{2,3,1,0:T(8,128)}, s32[1,3,100,32]{2,3,1,0:T(8,128)S(1)}, u32[]{:S(2)}) copy-start(s32[1,3,100,32]{2,3,1,0:T(8,128)S(1)} %get-tuple-element.180) | copy-start | bytes 115204
  209.2 46.4 %copy-start.85 = (s32[1,3,100,32]{2,3,1,0:T(8,128)}, s32[1,3,100,32]{2,3,1,0:T(8,128)S(1)}, u32[]{:S(2)}) copy-start(s32[1,3,100,32]{2,3,1,0:T(8,128)S(1)} %get-tuple-element.178) | copy-start | bytes 115204
  217.9 42.6 %copy-start.161 = (f32[256]{0:T(256)}, f32[256]{0:T(256)S(1)}, u32[]{:S(2)}) copy-start(f32[256]{0:T(256)S(1)} %compare_convert_fusion.4) | copy-start | bytes 3076
  259.8 358.5 %all-reduce.23.cloned.1.call-start = ((), (), s32[]{:S(2)}) async-start(), calls=%async_computation.10 | async-start | bytes 786432 | tf_op jit(solution)/shard_map/psum | solution.py:36
  260.4 156.5 %copy-start.159 = (f32[256]{0:T(256)}, f32[256]{0:T(256)S(1)}, u32[]{:S(2)}) copy-start(f32[256]{0:T(256)S(1)} %compare_convert_fusion.3) | copy-start | bytes 3076
  306.2 51.3 %copy-start.114 = (s32[3,100,32,1]{1,2,3,0:T(8,128)S(1)}, s32[3,100,32,1]{1,2,3,0:T(8,128)}, u32[]{:S(2)}) copy-start(s32[3,100,32,1]{1,2,3,0:T(8,128)} %get-tuple-element.125) | copy-start | bytes 115204
  306.2 51.6 %copy-start.172 = (s32[1,3,256]{2,0,1:T(1,128)S(1)}, s32[1,3,256]{2,0,1:T(1,128)}, u32[]{:S(2)}) copy-start(s32[1,3,256]{2,0,1:T(1,128)} %get-tuple-element.199) | copy-start | bytes 9220
  306.2 51.6 %copy-start.113 = (s32[3,100,32,1]{1,2,3,0:T(8,128)S(1)}, s32[3,100,32,1]{1,2,3,0:T(8,128)}, u32[]{:S(2)}) copy-start(s32[3,100,32,1]{1,2,3,0:T(8,128)} %get-tuple-element.181) | copy-start | bytes 115204
  306.2 112.2 %collective-permute-start = (bf16[256,768]{1,0:T(8,128)(2,1)}, bf16[256,768]{1,0:T(8,128)(2,1)S(1)}, u32[]{:S(2)}, u32[]{:S(2)}) collective-permute-start(bf16[256,768]{1,0:T(8,128)(2,1)} %get-tuple-element.127), channel_id=1, source_target_pairs={{0,16},{1,17},{2,18},{3,19},{4,20},{5,21},{6,22},{7,23},{8,24},{9,... | collective-permute-start | bytes 1179656 | tf_op jit(solution)/shard_map/ppermute | solution.py:14
  308.2 49.8 %copy-start.171 = (s32[1,3,256]{2,0,1:T(1,128)S(1)}, s32[1,3,256]{2,0,1:T(1,128)}, u32[]{:S(2)}) copy-start(s32[1,3,256]{2,0,1:T(1,128)} %get-tuple-element.197) | copy-start | bytes 9220
  357.5 50.4 %copy-start.170 = (s32[1,3,256]{2,0,1:T(1,128)S(1)}, s32[1,3,256]{2,0,1:T(1,128)}, u32[]{:S(2)}) copy-start(s32[1,3,256]{2,0,1:T(1,128)} %get-tuple-element.198) | copy-start | bytes 9220
  358.0 57.5 %copy-start.169 = (s32[1,3,256]{2,0,1:T(1,128)S(1)}, s32[1,3,256]{2,0,1:T(1,128)}, u32[]{:S(2)}) copy-start(s32[1,3,256]{2,0,1:T(1,128)} %get-tuple-element.202) | copy-start | bytes 9220
  358.2 59.5 %copy-start.41 = (f32[256,576]{0,1:S(1)}, f32[256,576]{0,1}, u32[]{:S(2)}) copy-start(f32[256,576]{0,1} %copy-done.40) | copy-start | bytes 1769476
  407.9 415.7 %copy-start.107 = (s32[1,3,256]{2,1,0:T(4,128)}, s32[1,3,256]{2,1,0:T(4,128)S(1)}, u32[]{:S(2)}) copy-start(s32[1,3,256]{2,1,0:T(4,128)S(1)} %copy.249) | copy-start | bytes 9220
  419.8 22.2 %copy-start.162 = (f32[256]{0:T(256)S(1)}, f32[256]{0:T(256)}, u32[]{:S(2)}) copy-start(f32[256]{0:T(256)} %copy-done.161) | copy-start | bytes 3076
  421.7 20.4 %copy-start.98 = (bf16[256,1,192]{0,2,1:T(8,128)(2,1)}, bf16[256,1,192]{0,2,1:T(8,128)(2,1)S(1)}, u32[]{:S(2)}) copy-start(bf16[256,1,192]{0,2,1:T(8,128)(2,1)S(1)} %get-tuple-element.166) | copy-start | bytes 294916
  442.1 25.6 %copy-start.31 = (bf16[3,1024,128]{1,2,0:T(8,128)(2,1)}, bf16[3,1024,128]{1,2,0:T(8,128)(2,1)S(1)}, u32[]{:S(2)}) copy-start(bf16[3,1024,128]{1,2,0:T(8,128)(2,1)S(1)} %all_gather.10) | copy-start | bytes 2359300
  576.8 91.4 %all-reduce.25.cloned.1.call-start = ((), (), s32[]{:S(2)}) async-start(), calls=%async_computation.11 | async-start | bytes 786432 | tf_op jit(solution)/shard_map/psum | solution.py:36
  619.5 48.6 %copy-start.7 = (f32[256,768]{1,0:T(8,128)}, f32[256,768]{1,0:T(8,128)S(1)}, u32[]{:S(2)}) copy-start(f32[256,768]{1,0:T(8,128)S(1)} %get-tuple-element.124) | copy-start | bytes 2359300
  623.9 48.0 %copy-start.110 = (bf16[3,100,64]{1,2,0:T(8,128)(2,1)S(1)}, bf16[3,100,64]{1,2,0:T(8,128)(2,1)}, u32[]{:S(2)}) copy-start(bf16[3,100,64]{1,2,0:T(8,128)(2,1)} %get-tuple-element.103) | copy-start | bytes 115204
  623.9 48.0 %copy-start.141 = (f32[3,100]{1,0:T(4,128)S(1)}, f32[3,100]{1,0:T(4,128)}, u32[]{:S(2)}) copy-start(f32[3,100]{1,0:T(4,128)} %copy-done.140) | copy-start | bytes 3604
  623.9 273.8 %all-reduce.27.cloned.1.call-start = ((), (), s32[]{:S(2)}) async-start(), calls=%async_computation.12 | async-start | bytes 786432 | tf_op jit(solution)/shard_map/psum | solution.py:36
  670.4 3.1 collective-permute-start.1
  675.0 21.4 %copy-start.50 = (bf16[256,768]{1,0:T(8,128)(2,1)}, bf16[256,768]{1,0:T(8,128)(2,1)S(1)}, u32[]{:S(2)}) copy-start(bf16[256,768]{1,0:T(8,128)(2,1)S(1)} %multiply_convert_fusion.4) | copy-start | bytes 1179652
  675.5 39.7 %copy-start.184 = (pred[1024]{0:T(1024)(128)(4,1)S(1)}, pred[1024]{0:T(1024)(128)(4,1)}, u32[]{:S(2)}) copy-start(pred[1024]{0:T(1024)(128)(4,1)} %get-tuple-element.243) | copy-start | bytes 3076
  676.5 40.2 %copy-start.15 = (f32[3,100,1024]{2,1,0:T(8,128)S(1)}, f32[3,100,1024]{2,1,0:T(8,128)}, u32[]{:S(2)}) copy-start(f32[3,100,1024]{2,1,0:T(8,128)} %reshape.804) | copy-start | bytes 3686404
  717.4 115.7 %copy-start.148 = (f32[3,100]{1,0:T(4,128)}, f32[3,100]{1,0:T(4,128)S(1)}, u32[]{:S(2)}) copy-start(f32[3,100]{1,0:T(4,128)S(1)} %get-tuple-element.65) | copy-start | bytes 3604
  717.4 136.2 %copy-start.147 = (f32[3,100]{1,0:T(4,128)}, f32[3,100]{1,0:T(4,128)S(1)}, u32[]{:S(2)}) copy-start(f32[3,100]{1,0:T(4,128)S(1)} %get-tuple-element.64) | copy-start | bytes 3604
  717.9 135.6 %copy-start.102 = (f32[3,100,64]{1,2,0:T(8,128)}, f32[3,100,64]{1,2,0:T(8,128)S(1)}, u32[]{:S(2)}) copy-start(f32[3,100,64]{1,2,0:T(8,128)S(1)} %fusion.296) | copy-start | bytes 230404
  720.2 97.0 %copy-start.76 = (bf16[256,1,192]{0,2,1:T(8,128)(2,1)}, bf16[256,1,192]{0,2,1:T(8,128)(2,1)S(1)}, u32[]{:S(2)}) copy-start(bf16[256,1,192]{0,2,1:T(8,128)(2,1)S(1)} %get-tuple-element.159) | copy-start | bytes 294916
  855.0 96.4 %all-reduce.29.cloned.1.call-start = ((), (), s32[]{:S(2)}) async-start(), calls=%async_computation.13 | async-start | bytes 786432 | tf_op jit(solution)/shard_map/psum | solution.py:40
  907.2 236.4 %reduce-scatter.15.cloned.1.call-start = ((), (), s32[]{:S(2)}) async-start(), calls=%async_computation.14 | async-start | bytes 983040 | tf_op jit(solution)/shard_map/reduce_scatter | solution.py:274
  1111.4 81.5 %all-reduce.31.cloned.1.call-start = ((), (), s32[]{:S(2)}) async-start(), calls=%async_computation.15 | async-start | bytes 786432 | tf_op jit(solution)/shard_map/psum | solution.py:40
  1150.0 104.8 %all-reduce.33.cloned.1.call-start = ((), (), s32[]{:S(2)}) async-start(), calls=%async_computation.16 | async-start | bytes 786432 | tf_op jit(solution)/shard_map/psum | solution.py:40
  1197.4 8.3 collective-permute-start.2
  1209.8 238.2 %reduce-scatter.17.cloned.1.call-start = ((), (), s32[]{:S(2)}) async-start(), calls=%async_computation.17 | async-start | bytes 983040 | tf_op jit(solution)/shard_map/reduce_scatter | solution.py:274
  1414.9 81.9 %all-reduce.35.cloned.1.call-start = ((), (), s32[]{:S(2)}) async-start(), calls=%async_computation.18 | async-start | bytes 786432 | tf_op jit(solution)/shard_map/psum | solution.py:40
  1448.0 48.8 %copy-start.151 = (f32[256]{0:T(256)S(1)}, f32[256]{0:T(256)}, u32[]{:S(2)}) copy-start(f32[256]{0:T(256)} %broadcast_multiply_fusion.8) | copy-start | bytes 3076
  1454.4 99.6 %all-reduce.37.cloned.1.call-start = ((), (), s32[]{:S(2)}) async-start(), calls=%async_computation.19 | async-start | bytes 786432 | tf_op jit(solution)/shard_map/psum | solution.py:40
  1501.3 3.7 collective-permute-start.3
  1508.0 46.1 %copy-start.168 = (f32[256]{0:T(256)S(1)}, f32[256]{0:T(256)}, u32[]{:S(2)}) copy-start(f32[256]{0:T(256)} %broadcast_multiply_fusion.5) | copy-start | bytes 3076
  1509.3 237.0 %reduce-scatter.19.cloned.1.call-start = ((), (), s32[]{:S(2)}) async-start(), calls=%async_computation.20 | async-start | bytes 983040 | tf_op jit(solution)/shard_map/reduce_scatter | solution.py:274
  1712.4 88.2 %all-reduce.39.cloned.1.call-start = ((), (), s32[]{:S(2)}) async-start(), calls=%async_computation.26 | async-start | bytes 1572864 | tf_op jit(solution)/shard_map/psum | solution.py:36
  1752.8 72.0 %reduce-scatter.27.cloned.1.call-start = ((), (), s32[]{:S(2)}) async-start(), calls=%async_computation.24 | async-start | bytes 491520
  1759.6 94.1 %reduce-scatter.23.cloned.1.call-start = ((), (), s32[]{:S(2)}) async-start(), calls=%async_computation.22 | async-start | bytes 1474560 | tf_op jit(solution)/shard_map/reduce_scatter | solution.py:413
  1764.6 109.8 %reduce-scatter.29.cloned.1.call-start = ((), (), s32[]{:S(2)}) async-start(), calls=%async_computation.25 | async-start | bytes 245760
  1770.3 32.1 %copy-start.174 = (f32[1,768]{1,0:T(1,128)S(1)}, f32[1,768]{1,0:T(1,128)}, u32[]{:S(2)}) copy-start(f32[1,768]{1,0:T(1,128)} %stack.267) | copy-start | bytes 9220
  1805.3 95.7 %reduce-scatter.25.cloned.1.call-start = ((), (), s32[]{:S(2)}) async-start(), calls=%async_computation.23 | async-start | bytes 1228800
  1816.5 114.7 %reduce-scatter.21.cloned.1.call-start = ((), (), s32[]{:S(2)}) async-start(), calls=%async_computation.21 | async-start | bytes 1474560 | tf_op jit(solution)/shard_map/reduce_scatter | solution.py:410
  1824.3 31.9 %copy-start.187 = (f32[256]{0:T(256)S(1)}, f32[256]{0:T(256)}, u32[]{:S(2)}) copy-start(f32[256]{0:T(256)} %get-tuple-element.75) | copy-start | bytes 3076
  1824.3 31.9 %copy-start.167 = (f32[256]{0:T(256)S(1)}, f32[256]{0:T(256)}, u32[]{:S(2)}) copy-start(f32[256]{0:T(256)} %broadcast_multiply_fusion.2) | copy-start | bytes 3076
  1824.3 31.9 %copy-start.177 = (f32[256]{0:T(256)S(1)}, f32[256]{0:T(256)}, u32[]{:S(2)}) copy-start(f32[256]{0:T(256)} %add_rsqrt_fusion) | copy-start | bytes 3076
  (158 other events, 555.0 us)
Sparse Core Ops, SparseCore 0:
  208.6 43.2 all-reduce.18
  259.9 44.0 all-reduce.20
  576.9 41.3 all-reduce.22
  624.0 44.0 all-reduce.24
  855.1 42.5 all-reduce.26
  907.3 44.0 all-reduce.28
  1111.6 21.1 reduce-scatter.14
  1150.2 42.7 all-reduce.30
  1209.9 44.8 all-reduce.32
  1415.0 20.9 reduce-scatter.16
  1454.6 42.2 all-reduce.34
  1509.4 44.6 all-reduce.36
  1712.5 20.8 reduce-scatter.18
  1752.9 47.5 all-reduce.38
  1802.7 20.5 reduce-scatter.26
  1826.1 27.4 reduce-scatter.22
  1856.3 18.0 reduce-scatter.28
  1876.7 24.3 reduce-scatter.24
  1903.4 27.7 reduce-scatter.20
where the time goes:
time: 1950 us; the launch traced here: 1940 us
  local copies, waits for them, and re-layouts  574 us (29%)
  waiting for transfers between devices  468 us (24%)
  other arithmetic  393 us (20%)
  matrix products  249 us (13%)
  blocking collectives  230 us (12%)
    gather x9, local copies, waits for them, and re-layouts, forward_layer(): lookup[where_at]  216 us
    unnamed x432, local copies, waits for them, and re-layouts  206 us
    psum x5, waiting for transfers between devices, grad_head_sum(): return lax.psum(values.astype(jnp.bfloat16), 'head').astype(jnp.float32)  201 us
    psum x6, waiting for transfers between devices, head_sum(): return lax.psum(values.astype(jnp.bfloat16), 'head').astype(jnp.float32)  175 us
    unnamed x11, other arithmetic  165 us
    psum x3, blocking collectives, backward_layer(): lax.psum(remote_part.astype(jnp.bfloat16), 'seq').astype(jnp.float32)  63.5 us
    psum x3, blocking collectives, forward_layer(): lax.psum(cluster_sums.astype(jnp.bfloat16), 'seq').astype(jnp.float32)  61.3 us
    psum x3, blocking collectives, backward_layer(): lax.psum((inv_root * jnp.einsum('hct,htd->hcd', grad_scores, key_local, p...  52.9 us
  transfers between devices with their start and end apart: 23, of which 16 were waited for; matrix products, arithmetic and copies ran while one was open for 16% of the time, Pallas kernels for 0%

commit v1 on v0

v1 whole, which is shorter than its diff:
```python
import functools

import jax
import jax.numpy as jnp
from jax import lax
from jax.experimental import pallas as pl
from jax.experimental.pallas import tpu as pltpu
from jax.sharding import PartitionSpec as P

epsilon = 1e-05
negative = -1e30
f32 = jnp.float32
bf16 = jnp.bfloat16
LANES = 128
HUBS = 64
DIRECT = 4


def round_up(value, step):
    return -(-value // step) * step


def iota(shape, dim):
    return lax.broadcasted_iota(jnp.int32, shape, dim)


def mm(a, b):
    return lax.dot_general(a, b, (((1,), (0,)), ((), ())), preferred_element_type=f32)


def mt(a, b):
    return lax.dot_general(a, b, (((1,), (1,)), ((), ())), preferred_element_type=f32)


def tm(a, b):
    return lax.dot_general(a, b, (((0,), (0,)), ((), ())), preferred_element_type=f32)


def parts2(v):
    high = v.astype(bf16)
    return high, (v - high.astype(f32)).astype(bf16)


def parts3(v):
    high = v.astype(bf16)
    rest = v - high.astype(f32)
    mid = rest.astype(bf16)
    return high.astype(f32), mid.astype(f32), rest - mid.astype(f32)


def pick_rows(one_hot, table):
    high, low = parts2(table)
    return mm(one_hot, high) + mm(one_hot, low)


def layer_stats(values):
    centred = values - jnp.mean(values, axis=-1, keepdims=True)
    inverse = lax.rsqrt(jnp.mean(centred * centred, axis=-1, keepdims=True) + epsilon)
    return centred * inverse, inverse


def norm_back(grad_hat, normed, inverse):
    return inverse * (
        grad_hat
        - jnp.mean(grad_hat, axis=-1, keepdims=True)
        - normed * jnp.mean(grad_hat * normed, axis=-1, keepdims=True)
    )


def columns(base_width, cols, rows):
    lane = iota((rows, base_width), 1)
    out = jnp.zeros((rows, base_width), f32)
    for at, col in enumerate(cols):
        out = jnp.where(lane == at, col, out)
    return out


def live_row(scal, rows):
    return (scal[1] + iota((1, rows), 1)) < scal[0]


def live_col(scal, rows):
    return (scal[1] + iota((rows, 1), 0)) < scal[0]


def table_t(cl_row, head, scal, clusters_pad):
    rows = cl_row.shape[1]
    same = iota((clusters_pad, rows), 0) == cl_row[head : head + 1, :]
    return (same & live_row(scal, rows)).astype(f32).astype(bf16)


def table(cl_col, head, clusters_pad):
    rows = cl_col.shape[0]
    same = iota((rows, clusters_pad), 1) == cl_col[:, head : head + 1]
    return same.astype(f32).astype(bf16)


def rolled(values, scal):
    return pltpu.roll(values.astype(f32), scal[2], 1).astype(bf16)


def summed(four):
    top_a, top_b, low_a, low_b = four
    return jnp.concatenate(
        [
            top_a[...].astype(f32) + top_b[...].astype(f32),
            low_a[...].astype(f32) + low_b[...].astype(f32),
        ],
        axis=0,
    )


def halves(values, top, low):
    half = values.shape[0] // 2
    top[...] = values[:half].astype(bf16)
    low[...] = values[half:].astype(bf16)


def call(kernel, outs, scal, args, flops=0):
    vmem = pl.BlockSpec(memory_space=pltpu.VMEM)
    moved = sum(a.size * a.dtype.itemsize for a in args) + sum(
        o.size * o.dtype.itemsize for o in outs
    )
    return pl.pallas_call(
        kernel,
        out_shape=outs,
        in_specs=[pl.BlockSpec(memory_space=pltpu.SMEM)] + [vmem] * len(args),
        out_specs=[vmem] * len(outs),
        compiler_params=pltpu.CompilerParams(vmem_limit_bytes=48 * 1024 * 1024),
        cost_estimate=pl.CostEstimate(flops=flops, bytes_accessed=moved, transcendentals=0),
    )(scal, *args)


def shaped(shape, dtype=f32):
    return jax.ShapeDtypeStruct(tuple(shape), dtype)


def prep_kernel(heads, slots, clusters_pad, total_rows, scal, flat, own_pick, in_list):
    entries = flat.shape[1]
    rows = own_pick.shape[1]
    per_head = entries // heads
    high_rows = round_up(max(total_rows // LANES, 1), 16)
    position = flat[...]
    high_hot = (iota((high_rows, entries), 0) == position // LANES).astype(f32).astype(bf16)
    low_hot = (iota((LANES, entries), 0) == position % LANES).astype(f32).astype(bf16)
    named = mt(high_hot, low_hot) > 0.5
    mask = named.astype(f32).astype(bf16)
    upper = (iota((LANES, LANES), 0) <= iota((LANES, LANES), 1)).astype(f32).astype(bf16)
    before = (iota((high_rows, high_rows), 1) < iota((high_rows, high_rows), 0)).astype(f32)
    rank = mm(mask, upper) + jnp.sum(mm(before.astype(bf16), mask), axis=1, keepdims=True)
    rank = jnp.where(named, rank, 0.0)
    first = scal[1] // LANES
    at_row = iota((high_rows, LANES), 0)
    own = jnp.concatenate(
        [
            jnp.sum(jnp.where(at_row == first + r, rank, 0.0), axis=0, keepdims=True)
            for r in range(rows // LANES)
        ],
        axis=1,
    )
    hub_row = iota((HUBS, rows), 0).astype(f32) + 1.0
    own_pick[...] = (hub_row == own).astype(f32).astype(bf16)
    by_low = tm(rank.astype(bf16), high_hot)
    hub_of = jnp.sum(by_low * low_hot.astype(f32), axis=0, keepdims=True)
    hub_hot = (iota((HUBS, entries), 0).astype(f32) + 1.0 == hub_of).astype(f32).astype(bf16)
    owner = iota((clusters_pad, per_head), 1) // slots
    owner_hot = (owner == iota((clusters_pad, per_head), 0)).astype(f32).astype(bf16)
    for h in range(heads):
        in_list[h] = mt(owner_hot, hub_hot[:, h * per_head : (h + 1) * per_head]).astype(bf16)


def project_kernel(first, heads, size, cl_pad, cl_rows, scal, *refs):
    if first:
        source, gains, w_qkv, cl_row, own_pick = refs[:5]
        n1r, q, k, v, pay = refs[5:]
        x = source[...].astype(f32)
    else:
        source, *four = refs[:5]
        gains, w_qkv, cl_row, own_pick = refs[5:9]
        y, n1r, q, k, v, pay = refs[9:]
        x = source[...] + summed(four)
        y[...] = x
    hat, _ = layer_stats(x)
    n1 = (hat * gains[0:1, :]).astype(bf16)
    qv = mm(n1, w_qkv[0]).astype(bf16)
    kv = mm(n1, w_qkv[1]).astype(bf16)
    vv = mm(n1, w_qkv[2]).astype(bf16)
    q[...] = qv
    k[...] = kv
    v[...] = vv
    sums, counts = [], []
    for h in range(heads):
        members = table_t(cl_row, h, scal, cl_pad)
        sums.append(mm(members, qv[:, h * size : (h + 1) * size]))
        counts.append(jnp.sum(members.astype(f32), axis=1, keepdims=True))
    width = heads * size
    spare = round_up(width + 1, LANES) - width
    block = jnp.concatenate(sums + [columns(spare, counts, cl_pad)], axis=1).astype(bf16)
    put_blocks(pay, 0, block, cl_rows)
    both = jnp.concatenate([mm(own_pick[...], kv), mm(own_pick[...], vv)], axis=1).astype(bf16)
    put_blocks(pay, cl_rows * (block.shape[1] // LANES), both, HUBS)
    n1r[...] = rolled(n1, scal)


def put_blocks(ref, start, block, rows):
    for at in range(block.shape[1] // LANES):
        ref[start + at * rows : start + (at + 1) * rows, :] = block[
            :rows, at * LANES : (at + 1) * LANES
        ]


def get_blocks(values, start, rows, count):
    return jnp.concatenate(
        [values[start + at * rows : start + (at + 1) * rows] for at in range(count)], axis=1
    )


def total_of(refs, start, rows, count):
    total = None
    for ref in refs:
        piece = ref[start : start + rows * count, :].astype(f32)
        total = piece if total is None else total + piece
    return get_blocks(total, 0, rows, count)


def pad_rows(values, rows):
    extra = rows - values.shape[0]
    if extra == 0:
        return values
    return jnp.concatenate([values, jnp.zeros((extra, values.shape[1]), values.dtype)], axis=0)


def centroid_kernel(count, heads, size, cl_pad, cl_rows, scal, *refs):
    pays = refs[:count]
    k, v, in_list, own_pick, centre_ref, cnt_ref, pay = refs[count:]
    width = heads * size
    blocks = round_up(width + 1, LANES) // LANES
    total = pad_rows(total_of(pays, 0, cl_rows, blocks), cl_pad)
    cnt_ref[...] = total[:, (blocks - 1) * LANES :]
    rows = k.shape[0]
    live = live_row(scal, rows)
    inv_root = size ** (-0.5)
    carried, extras = [], []
    for h in range(heads):
        cnt = total[:, width + h : width + h + 1]
        centre = jnp.where(
            cnt > 0, total[:, h * size : (h + 1) * size] / jnp.maximum(cnt, 1.0), 0.0
        ).astype(bf16)
        centre_ref[h] = centre
        scores = mt(centre, k[:, h * size : (h + 1) * size]) * inv_root
        peak = jnp.max(jnp.where(live, scores, negative), axis=1, keepdims=True)
        weighted = jnp.where(live, jnp.exp(jnp.where(live, scores - peak, 0.0)), 0.0)
        in_top = mm(in_list[h], own_pick[...])
        mass = jnp.sum(weighted, axis=1, keepdims=True)
        top_mass = jnp.sum(weighted * in_top, axis=1, keepdims=True)
        rest = (weighted * (1.0 - in_top)).astype(bf16)
        carried.append(mm(rest, v[:, h * size : (h + 1) * size]))
        for value in (peak, mass, top_mass):
            extras.extend(parts3(value))
    spare = blocks * LANES - width
    block = jnp.concatenate(carried + [columns(spare, extras, cl_pad)], axis=1).astype(bf16)
    put_blocks(pay, 0, block, cl_rows)


def member_kernel(count, heads, size, cl_pad, cl_rows, scal, *refs):
    pays = refs[:count]
    q, cl_col, in_list, hub_ref, prob_ref, top_ref = refs[count:]
    width = heads * size
    blocks = round_up(width + 1, LANES) // LANES
    hub = total_of(pays, blocks * cl_rows, HUBS, 2 * width // LANES).astype(bf16)
    hub_ref[...] = hub
    inv_root = size ** (-0.5)
    probs, outs = [], []
    for h in range(heads):
        keys = hub[:, h * size : (h + 1) * size]
        values = hub[:, width + h * size : width + (h + 1) * size]
        logits = mt(q[:, h * size : (h + 1) * size], keys) * inv_root
        chosen = mm(table(cl_col, h, cl_pad), in_list[h]) > 0.5
        logits = jnp.where(chosen, logits, negative)
        exponent = jnp.where(
            chosen, jnp.exp(logits - jnp.max(logits, axis=1, keepdims=True)), 0.0
        )
        prob = exponent / jnp.sum(exponent, axis=1, keepdims=True)
        probs.append(prob)
        outs.append(mm(prob.astype(bf16), values))
    prob_ref[...] = jnp.concatenate(probs, axis=1)
    top_ref[...] = jnp.concatenate(outs, axis=1)


def combine_kernel(count, heads, size, cl_pad, cl_rows, scal, *refs):
    pays = refs[:count]
    top_out, cl_col, att_ref, stat_ref = refs[count:]
    width = heads * size
    blocks = round_up(width + 1, LANES) // LANES
    tables = [
        pad_rows(get_blocks(ref[...].astype(f32), 0, cl_rows, blocks), cl_pad) for ref in pays
    ]
    rows = top_out.shape[0]
    live = live_col(scal, rows)
    pieces = []
    for h in range(heads):

        def value(one, which):
            at = width + 9 * h + 3 * which
            return one[:, at : at + 1] + one[:, at + 1 : at + 2] + one[:, at + 2 : at + 3]

        peaks = [value(one, 0) for one in tables]
        peak = functools.reduce(jnp.maximum, peaks)
        mass = top_mass = carried = 0.0
        for one, mine in zip(tables, peaks):
            scale = jnp.exp(mine - peak)
            mass = mass + value(one, 1) * scale
            top_mass = top_mass + value(one, 2) * scale
            carried = carried + one[:, h * size : (h + 1) * size] * scale
        safe = jnp.where(mass > 0, mass, 1.0)
        remote = carried / safe
        share = top_mass / safe
        lanes = LANES - size
        stat_ref[h] = jnp.concatenate(
            [carried, columns(lanes, (peak, safe, top_mass, share), cl_pad)], axis=1
        )
        looked = pick_rows(
            table(cl_col, h, cl_pad),
            jnp.concatenate([remote, columns(lanes, (share,), cl_pad)], axis=1),
        )
        att = looked[:, size : size + 1] * top_out[:, h * size : (h + 1) * size] + looked[:, :size]
        pieces.append(jnp.where(live, att, 0.0))
    joined = jnp.concatenate(pieces, axis=1).astype(bf16)
    att_ref[...] = joined


def feed_kernel(count, scal, *refs):
    source = refs[0]
    atts = refs[1 : 1 + count]
    w_out, gains, w_in, w_back = refs[1 + count : 5 + count]
    x1_ref, n2r, active_ref, slope_ref, top, low = refs[5 + count :]
    x1 = source[...].astype(f32)
    for at, ref in enumerate(atts):
        x1 = x1 + mm(ref[...], w_out[at])
    x1_ref[...] = x1
    hat, _ = layer_stats(x1)
    n2 = (hat * gains[1:2, :]).astype(bf16)
    hidden = mm(n2, w_in[...])
    root = (2.0 / 3.141592653589793) ** 0.5
    square = hidden * hidden
    bent = jnp.tanh(root * hidden * (1.0 + 0.044715 * square))
    active = (0.5 * hidden * (1.0 + bent)).astype(bf16)
    active_ref[...] = active
    slope_ref[...] = 0.5 * (1.0 + bent) + 0.5 * hidden * (1.0 - bent * bent) * root * (
        1.0 + 3 * 0.044715 * square
    )
    halves(mm(active, w_back[...]), top, low)
    n2r[...] = rolled(n2, scal)


def feed_back_kernel(last, scal, *refs):
    if last:
        cot, slope, w_in, w_back = refs[:4]
        dybr, dz_ref, top, low = refs[4:]
        dyb = cot[...]
    else:
        grad_middle, source, *four = refs[:6]
        gains, slope, w_in, w_back = refs[6:10]
        dy_ref, gain_ref, dybr, dz_ref, top, low = refs[10:]
        dy = input_grad(grad_middle, source, four, gains, gain_ref)
        dy_ref[...] = dy
        dyb = dy.astype(bf16)
    dz = (mt(dyb, w_back[...]) * slope[...]).astype(bf16)
    dz_ref[...] = dz
    halves(mt(dz, w_in[...]), top, low)
    dybr[...] = rolled(dyb, scal)


def input_grad(grad_middle, source, four, gains, gain_ref):
    grad_normed = summed(four)
    hat, inverse = layer_stats(source[...].astype(f32))
    gain_ref[...] = jnp.sum(grad_normed * hat, axis=0, keepdims=True)
    return grad_middle[...] + norm_back(grad_normed * gains[0:1, :], hat, inverse)


def input_grad_kernel(scal, *refs):
    grad_middle, source, *four = refs[:6]
    gains, dy_ref, gain_ref = refs[6:]
    dy_ref[...] = input_grad(grad_middle, source, four, gains, gain_ref)


def middle_back_kernel(heads, size, cl_pad, cl_rows, scal, *refs):
    four = refs[:4]
    middle, grad_out, gains, w_out, top_out, cl_row = refs[4:10]
    dx1_ref, dx1r, dtop_ref, gain_ref, pay = refs[10:]
    grad_normed = summed(four)
    hat, inverse = layer_stats(middle[...])
    gain_ref[...] = jnp.sum(grad_normed * hat, axis=0, keepdims=True)
    dx1 = grad_out[...].astype(f32) + norm_back(grad_normed * gains[1:2, :], hat, inverse)
    dx1_ref[...] = dx1
    dx1b = dx1.astype(bf16)
    rows = dx1.shape[0]
    datt = mt(dx1b, w_out[...])
    dtop = jnp.where(live_col(scal, rows), datt, 0.0).astype(bf16)
    dtop_ref[...] = dtop
    sums, shares = [], []
    for h in range(heads):
        members = table_t(cl_row, h, scal, cl_pad)
        own = dtop[:, h * size : (h + 1) * size]
        sums.append(mm(members, own))
        product = own.astype(f32) * top_out[:, h * size : (h + 1) * size]
        both = mm(members, jnp.concatenate(parts2(product), axis=1))
        shares.extend(parts3(jnp.sum(both, axis=1, keepdims=True)))
    width = heads * size
    spare = round_up(width + 1, LANES) - width
    block = jnp.concatenate(sums + [columns(spare, shares, cl_pad)], axis=1).astype(bf16)
    put_blocks(pay, 0, block, cl_rows)
    dx1r[...] = rolled(dx1b, scal)


def member_back_kernel(heads, size, cl_pad, scal, *refs):
    q, hub_ref, prob_ref, dtop, stat, cl_col, dq_ref, pay = refs
    width = heads * size
    inv_root = size ** (-0.5)
    hub = hub_ref[...]
    dqs, dks, dvs = [], [], []
    for h in range(heads):
        keys = hub[:, h * size : (h + 1) * size]
        values = hub[:, width + h * size : width + (h + 1) * size]
        prob = prob_ref[:, h * HUBS : (h + 1) * HUBS]
        own = dtop[:, h * size : (h + 1) * size]
        share = pick_rows(table(cl_col, h, cl_pad), stat[h])[:, size + 3 : size + 4]
        da = mt(own, values) * share
        dg = (prob * (da - jnp.sum(prob * da, axis=1, keepdims=True))).astype(bf16)
        dqs.append(mm(dg, keys) * inv_root)
        dks.append(tm(dg, q[:, h * size : (h + 1) * size]) * inv_root)
        scaled = own.astype(f32) * share
        dvs.append(tm(prob.astype(bf16), scaled.astype(bf16)))
    dq_ref[...] = jnp.concatenate(dqs, axis=1)
    put_blocks(pay, 0, jnp.concatenate(dks + dvs, axis=1).astype(bf16), HUBS)


def centroid_back_kernel(count, heads, size, cl_pad, cl_rows, scal, *refs):
    pays = refs[:count]
    centre_ref, stat, k, v, in_list, own_pick, pay, dk_ref, dv_ref = refs[count:]
    width = heads * size
    blocks = round_up(width + 1, LANES) // LANES
    total = pad_rows(total_of(pays, 0, cl_rows, blocks), cl_pad)
    rows = k.shape[0]
    live = live_row(scal, rows)
    inv_root = size ** (-0.5)
    dcs, dks, dvs = [], [], []
    for h in range(heads):
        keys = k[:, h * size : (h + 1) * size]
        values = v[:, h * size : (h + 1) * size]
        centre = centre_ref[h]
        grad_remote = total[:, h * size : (h + 1) * size]
        at = width + 3 * h
        grad_share = total[:, at : at + 1] + total[:, at + 1 : at + 2] + total[:, at + 2 : at + 3]
        carried = stat[h][:, :size]
        peak = stat[h][:, size : size + 1]
        mass = stat[h][:, size + 1 : size + 2]
        top_mass = stat[h][:, size + 2 : size + 3]
        grad_carried = (grad_remote / mass).astype(bf16)
        grad_top = grad_share / mass
        grad_mass = -(
            jnp.sum(grad_remote * carried, axis=1, keepdims=True) + grad_share * top_mass
        ) / (mass * mass)
        scores = mt(centre, keys) * inv_root
        weighted = jnp.where(live, jnp.exp(jnp.where(live, scores - peak, 0.0)), 0.0)
        in_top = mm(in_list[h], own_pick[...])
        rest = (weighted * (1.0 - in_top)).astype(bf16)
        grad_weighted = (
            (1.0 - in_top) * mt(grad_carried, values) + in_top * grad_top + grad_mass
        )
        grad_scores = (grad_weighted * weighted).astype(bf16)
        dcs.append(mm(grad_scores, keys) * inv_root)
        dks.append(tm(grad_scores, centre) * inv_root)
        dvs.append(tm(rest, grad_carried))
    spare = blocks * LANES - width
    block = jnp.concatenate(dcs + [jnp.zeros((cl_pad, spare), f32)], axis=1).astype(bf16)
    put_blocks(pay, 0, block, cl_rows)
    dk_ref[...] = jnp.concatenate(dks, axis=1)
    dv_ref[...] = jnp.concatenate(dvs, axis=1)


def project_back_kernel(count, heads, size, cl_pad, cl_rows, scal, *refs):
    centre_pays = refs[:count]
    hub_pays = refs[count : 2 * count]
    dq_top, dk_c, dv_c, cnt_ref, cl_col, own_pick, w_qkv = refs[2 * count : 2 * count + 7]
    dqkv_ref, top, low = refs[2 * count + 7 :]
    width = heads * size
    blocks = round_up(width + 1, LANES) // LANES
    total = pad_rows(total_of(centre_pays, 0, cl_rows, blocks), cl_pad)
    hub = total_of(hub_pays, 0, HUBS, 2 * width // LANES)
    high, low_part = parts2(hub)
    spread = tm(own_pick[...], high) + tm(own_pick[...], low_part)
    rows = dq_top.shape[0]
    live = live_col(scal, rows)
    base = round_up(width + 1, LANES) - LANES
    dqs = []
    for h in range(heads):
        at = width - base + h
        cnt = jnp.maximum(cnt_ref[:, at : at + 1], 1.0)
        from_centre = pick_rows(
            table(cl_col, h, cl_pad), total[:, h * size : (h + 1) * size] / cnt
        )
        dqs.append(jnp.where(live, from_centre, 0.0))
    dq = (dq_top[...] + jnp.concatenate(dqs, axis=1)).astype(bf16)
    dk = (dk_c[...] + spread[:, :width]).astype(bf16)
    dv = (dv_c[...] + spread[:, width:]).astype(bf16)
    dqkv_ref[...] = jnp.concatenate([dq, dk, dv], axis=1)
    halves(mt(dq, w_qkv[0]) + mt(dk, w_qkv[1]) + mt(dv, w_qkv[2]), top, low)


def moved(block, axis, target):
    devices = range(lax.axis_size(axis))
    return lax.ppermute(block, axis, [(i, target(i)) for i in devices])


def swap(block):
    return moved(block, "section", lambda i: i ^ 1)


def every_seq(block):
    count = lax.axis_size("seq")
    if count > DIRECT:
        gathered = lax.all_gather(block, "seq")
        return [gathered[at] for at in range(count)]
    return [block] + [
        moved(block, "seq", lambda i, k=k: (i + k) % count) for k in range(1, count)
    ]


def every_head(block):
    return [block] + [
        moved(block, "head", lambda i, k=k: i ^ k) for k in range(1, lax.axis_size("head"))
    ]


def head_sum(top, low):
    distances = [1 << at for at in range(lax.axis_size("head").bit_length() - 1)]
    for step in range(len(distances)):
        one = distances[step]
        other = distances[len(distances) - 1 - step]
        far_top = moved(top, "head", lambda i: i ^ one)
        far_low = moved(low, "head", lambda i: i ^ other)
        if step < len(distances) - 1:
            top = (top.astype(f32) + far_top.astype(f32)).astype(bf16)
            low = (low.astype(f32) + far_low.astype(f32)).astype(bf16)
    return (top, far_top, low, far_low)


def to_owner(block, layer):
    far = lax.ppermute(block, "section", [(1 - layer, layer)])
    return block.astype(f32) + far.astype(f32)


def over_seq(block, layer):
    count = lax.axis_size("seq")
    part = block.shape[0] // count
    if count > DIRECT:
        return lax.psum_scatter(block.astype(bf16), "seq", scatter_dimension=0, tiled=True).astype(
            f32
        )
    total = block[:part]
    for k in range(1, count):
        route = [
            (layer * count + i, layer * count + (i + k) % count) for i in range(count)
        ]
        piece = block[k * part : (k + 1) * part].astype(bf16)
        total = total + lax.ppermute(piece, ("section", "seq"), route).astype(f32)
    return total


def shards(tokens, cotangent, lengths, clusters, top_index, w_qkv, w_out, w_in, w_back, gains):
    section = lax.axis_index("section")
    me = lax.axis_index("seq")
    count = lax.axis_size("seq")
    pick = lambda array: lax.dynamic_index_in_dim(array, section, 0, keepdims=False)
    tok, cot, length = pick(tokens), pick(cotangent), pick(lengths)
    cl_row, tops = pick(clusters), pick(top_index)
    rows, dim = tok.shape
    heads, cluster_count, slots = tops.shape
    size = w_qkv.shape[3] // heads
    width = heads * size
    hidden = w_in.shape[2]
    total_rows = rows * count
    cl_pad = round_up(cluster_count, LANES)
    cl_rows = round_up(cluster_count, 16)
    shift = lax.rem(dim - me * (dim // count), dim) if count <= DIRECT else 0
    scal = jnp.stack([length, me * rows, jnp.asarray(shift, jnp.int32)]).astype(jnp.int32)
    cl_col = cl_row.T
    blocks = round_up(width + 1, LANES) // LANES
    hub_blocks = 2 * width // LANES
    sizes = (heads, size, cl_pad, cl_rows)
    fours = [shaped((rows // 2, dim), bf16)] * 2

    def both_layers(mine):
        other = swap(mine)
        return [jnp.where(section == layer, mine, other) for layer in range(2)]

    w_qkv = both_layers(w_qkv[0])
    out_all = both_layers(jnp.stack(every_head(w_out[0])))
    w_in = both_layers(w_in[0])
    w_back = both_layers(w_back[0])
    gains = [g.astype(f32) for g in both_layers(gains[0])]

    own_pick, in_list = call(
        functools.partial(prep_kernel, heads, slots, cl_pad, total_rows),
        [shaped((HUBS, rows), bf16), shaped((heads, cl_pad, HUBS), bf16)],
        scal,
        [tops.reshape(1, -1)],
    )

    source, four = tok, None
    kept, acts = [], []
    for layer in range(2):
        outs = [
            shaped((rows, dim), bf16),
            shaped((rows, width), bf16),
            shaped((rows, width), bf16),
            shaped((rows, width), bf16),
            shaped((blocks * cl_rows + hub_blocks * HUBS, LANES), bf16),
        ]
        tail = [gains[layer], w_qkv[layer], cl_row, own_pick]
        if layer == 0:
            n1r, q, k, v, pay = call(
                functools.partial(project_kernel, True, *sizes), outs, scal, [tok] + tail
            )
        else:
            source, n1r, q, k, v, pay = call(
                functools.partial(project_kernel, False, *sizes),
                [shaped((rows, dim))] + outs,
                scal,
                [x1, *four] + tail,
            )
            acts.append(source)
        pays = every_seq(pay)
        centre, cnt, pay = call(
            functools.partial(centroid_kernel, len(pays), *sizes),
            [
                shaped((heads, cl_pad, size), bf16),
                shaped((cl_pad, LANES)),
                shaped((blocks * cl_rows, LANES), bf16),
            ],
            scal,
            [*pays, k, v, in_list, own_pick],
        )
        stats = every_seq(pay)
        hub, prob, top_out = call(
            functools.partial(member_kernel, len(pays), *sizes),
            [
                shaped((HUBS, 2 * width), bf16),
                shaped((rows, heads * HUBS)),
                shaped((rows, width)),
            ],
            scal,
            [*pays, q, cl_col, in_list],
        )
        att, stat = call(
            functools.partial(combine_kernel, len(stats), *sizes),
            [shaped((rows, width), bf16), shaped((heads, cl_pad, LANES))],
            scal,
            [*stats, top_out, cl_col],
        )
        atts = every_head(att)
        x1, n2r, active, slope, top, low = call(
            functools.partial(feed_kernel, len(atts)),
            [
                shaped((rows, dim)),
                shaped((rows, dim), bf16),
                shaped((rows, hidden), bf16),
                shaped((rows, hidden)),
            ]
            + fours,
            scal,
            [source, *atts, out_all[layer], gains[layer], w_in[layer], w_back[layer]],
        )
        four = head_sum(top, low)
        kept.append(
            (source, n1r, q, k, v, centre, cnt, hub, prob, top_out, att, stat, x1, n2r, active, slope)
        )
    top_a, top_b, low_a, low_b = (piece.astype(f32) for piece in four)
    acts.append(x1 + jnp.concatenate([top_a + top_b, low_a + low_b], axis=0))

    in_grads, grads, gain_grads = [None, None], [None, None], [None, None]
    for layer in (1, 0):
        (source, n1r, q, k, v, centre, cnt, hub, prob, top_out, att, stat, x1, n2r, active, slope) = kept[layer]
        outs = [shaped((rows, dim), bf16), shaped((rows, hidden), bf16)] + fours
        tail = [slope, w_in[layer], w_back[layer]]
        if layer == 1:
            dy = cot
            dybr, dz, top, low = call(
                functools.partial(feed_back_kernel, True), outs, scal, [cot] + tail
            )
        else:
            dy, gain_one, dybr, dz, top, low = call(
                functools.partial(feed_back_kernel, False),
                [shaped((rows, dim)), shaped((1, dim))] + outs,
                scal,
                [dx1, kept[1][0], *four, gains[1]] + tail,
            )
            in_grads[1] = dy
            gain_grads[1] = jnp.concatenate([gain_one, gain_two], axis=0)
        four = head_sum(top, low)
        first = to_owner(tm(dybr, active).astype(bf16), layer)
        second = to_owner(tm(n2r, dz).astype(bf16), layer)
        dx1, dx1r, dtop, gain_two, pay = call(
            functools.partial(middle_back_kernel, *sizes),
            [
                shaped((rows, dim)),
                shaped((rows, dim), bf16),
                shaped((rows, width), bf16),
                shaped((1, dim)),
                shaped((blocks * cl_rows, LANES), bf16),
            ],
            scal,
            [*four, x1, dy, gains[layer], out_all[layer][0], top_out, cl_row],
        )
        pays = every_seq(pay)
        dq_top, hub_pay = call(
            functools.partial(member_back_kernel, heads, size, cl_pad),
            [shaped((rows, width)), shaped((hub_blocks * HUBS, LANES), bf16)],
            scal,
            [q, hub, prob, dtop, stat, cl_col],
        )
        hub_pays = every_seq(hub_pay)
        pay, dk, dv = call(
            functools.partial(centroid_back_kernel, len(pays), *sizes),
            [
                shaped((blocks * cl_rows, LANES), bf16),
                shaped((rows, width)),
                shaped((rows, width)),
            ],
            scal,
            [*pays, centre, stat, k, v, in_list, own_pick],
        )
        pays = every_seq(pay)
        dqkv, top, low = call(
            functools.partial(project_back_kernel, len(pays), *sizes),
            [shaped((rows, 3 * width), bf16)] + fours,
            scal,
            [*pays, *hub_pays, dq_top, dk, dv, cnt, cl_col, own_pick, w_qkv[layer]],
        )
        four = head_sum(top, low)
        third = jnp.concatenate([tm(n1r, dqkv), tm(dx1r, att)], axis=1)
        third = to_owner(third.astype(bf16), layer)
        grads[layer] = [over_seq(one, layer) for one in (first, second, third)]
    dy, gain_one = call(
        input_grad_kernel,
        [shaped((rows, dim)), shaped((1, dim))],
        scal,
        [dx1, tok, *four, gains[0]],
    )
    in_grads[0] = dy
    gain_grads[0] = jnp.concatenate([gain_one, gain_two], axis=0)

    def owned(pair):
        mine = jnp.where(section == 0, pair[0], pair[1])
        far = swap(jnp.where(section == 0, pair[1], pair[0]))
        return mine, far

    def stacked(pair):
        mine, far = owned(pair)
        return jnp.stack([jnp.where(section == 0, mine, far), jnp.where(section == 0, far, mine)])

    mine, far = owned(gain_grads)
    gain_sum = lax.psum_scatter(
        (mine + far), "seq", scatter_dimension=1, tiled=True
    ) if count > DIRECT else gain_over_seq(mine + far, me, count)
    back, into, rest = (jnp.where(section == 0, a, b) for a, b in zip(*grads))
    grad_qkv = rest[:, : 3 * width].reshape(-1, 3, width).transpose(1, 0, 2)
    grad_out = rest[:, 3 * width :].T
    return (
        stacked(acts)[None],
        stacked(in_grads)[None],
        grad_qkv[None],
        grad_out[None],
        into[None],
        back.T[None],
        gain_sum[None],
    )


def gain_over_seq(values, me, count):
    everyone = sum(every_seq(values))
    part = values.shape[1] // count
    return lax.dynamic_slice_in_dim(everyone, me * part, part, 1)


def solution(mesh):
    placed = (
        P(None, "seq", None),
        P(None, "seq", None),
        P(),
        P(None, "head", "seq"),
        P(None, "head", None, None),
        P("section", None, None, "head"),
        P("section", "head", None),
        P("section", None, "head"),
        P("section", "head", None),
        P("section", None, None),
    )
    return jax.shard_map(
        shards,
        mesh=mesh,
        in_specs=placed,
        out_specs=(
            P("section", None, "seq", None),
            P("section", None, "seq", None),
            P("section", None, "seq", "head"),
            P("section", "head", "seq"),
            P("section", "seq", "head"),
            P("section", "head", "seq"),
            P("section", None, "seq"),
        ),
        check_vma=False,
    )
```

time: 1950 us -> 402 us (0.21)
  local copies, waits for them, and re-layouts: 574 us -> 25.6 us
  other arithmetic: 393 us -> 47.7 us
  waiting for transfers between devices: 468 us -> 126 us
  matrix products: 249 us -> 4.53 us
  blocking collectives: 230 us -> 0 us
  starting transfers between devices: 8.05 us -> 141 us
  Pallas kernels: 0 us -> 48.6 us
    psum x11 -> x0, waiting for transfers between devices: 377 us -> none  [the longest x5 201 us: grad_head_sum(): return lax.psum(values.astype(jnp.bfloat16), 'head').astype(jnp.float32)]
    dot_general x99 -> x8, matrix products: 246 us -> 4.53 us  [tm(): lax.dot_general(a, b, (((0,), (0,)), ((), ())), preferred_element_type=f32)]
    gather x9 -> x0, local copies, waits for them, and re-layouts: 216 us -> none  [forward_layer(): lookup[where_at]]
    unnamed x432 -> x123, local copies, waits for them, and re-layouts: 206 us -> 11.7 us
    psum x9 -> x0, blocking collectives: 178 us -> none  [the longest x3 63.5 us: backward_layer(): lax.psum(remote_part.astype(jnp.bfloat16), 'seq').astype(jnp.float32)]
    unnamed x11 -> x0, other arithmetic: 165 us -> none
    ppermute x4 -> x98, starting transfers between devices: 5.59 us -> 141 us  [the longest x74 87.8 us: moved(): return lax.ppermute(block, axis, [(i, target(i)) for i in devices])]
    ppermute x4 -> x98, waiting for transfers between devices: 0.18 us -> 126 us  [the longest x74 84.8 us: moved(): return lax.ppermute(block, axis, [(i, target(i)) for i in devices])]
  transfers between devices with their start and end apart: 23 -> 98, of which waited for: 16 -> 40; matrix products, arithmetic and copies ran while one was open for 16% -> 18% of each run, Pallas kernels for 0% -> 8%
where the time goes in v1:
time: 402 us; the launch traced here: 395 us
  starting transfers between devices  141 us (35%)
  waiting for transfers between devices  126 us (31%)
  Pallas kernels  48.6 us (12%)
  other arithmetic  47.7 us (12%)
  local copies, waits for them, and re-layouts  25.6 us (6%)
  matrix products  4.53 us (1%)
    ppermute x74, starting transfers between devices, moved(): return lax.ppermute(block, axis, [(i, target(i)) for i in devices])  87.8 us
    ppermute x74, waiting for transfers between devices, moved(): return lax.ppermute(block, axis, [(i, target(i)) for i in devices])  84.8 us
    pallas_call x22, Pallas kernels, call(): pl.pallas_call(kernel, out_shape=outs, in_specs=[pl.BlockSpec(memory_spac...  48.6 us
    ppermute x18, starting transfers between devices, over_seq(): total = total + lax.ppermute(piece, ('section', 'seq'), route).astype(f32)  41.8 us
    ppermute x18, waiting for transfers between devices, over_seq(): total = total + lax.ppermute(piece, ('section', 'seq'), route).astype(f32)  41.2 us
    another operation x6, other arithmetic  13.1 us
    unnamed x123, local copies, waits for them, and re-layouts  11.7 us
    select_n x4, other arithmetic, both_layers(): return [jnp.where(section == layer, mine, other) for layer in range(2)]  11.2 us
  transfers between devices with their start and end apart: 98, of which 40 were waited for; matrix products, arithmetic and copies ran while one was open for 18% of the time, Pallas kernels for 8%

profile of v1, /device:TPU:0, one launch (start us, length us, event | category | flops | bytes accessed | tf_op | source)
XLA Modules:
  0.0 395.2 jit_solution(2128825854000797578)
XLA Ops:
  1.2 3.5 collective-permute-start.13
  9.2 2.4 copy.45
  12.0 4.3 %shard_map.153 = (bf16[64,256]{1,0:T(8,128)(2,1)S(1)}, bf16[3,128,64]{2,1,0:T(8,128)(2,1)S(1)}) custom-call(s32[3]{0:T(128)S(1)} %pad_add_fusion.scal, s32[1,9600]{1,0:T(1,128)S(1)} %reshape.21.flat), custom_call_target="tpu_custom_call" | custom-call | bytes 120320 | tf_op jit(solution)/shard_map/pallas_call | solution.py:124
  18.8 6.5 %collective-permute-done.11 = bf16[192,768]{1,0:T(8,128)(2,1)S(1)} collective-permute-done((bf16[192,768]{1,0:T(8,128)(2,1)S(1)}, bf16[192,768]{1,0:T(8,128)(2,1)S(1)}, u32[]{:S(2)}, u32[]{:S(2)}) %collective-permute-start.11) | collective-permute-done | bytes 294944 | tf_op jit(solution)/shard_map/ppermute | solution.py:513
  26.6 2.3 copy.47
  28.9 2.8 bitcast_select_fusion.1
  33.4 3.7 collective-permute-start.4
  37.0 3.3 collective-permute-done.4.refs_3_
  40.4 7.0 %collective-permute-done.3.refs_2_ = bf16[416,128]{1,0:T(8,128)(2,1)S(1)} collective-permute-done((bf16[416,128]{1,0:T(8,128)(2,1)S(1)}, bf16[416,128]{1,0:T(8,128)(2,1)S(1)}, u32[]{:S(2)}, u32[]{:S(2)}) %collective-permute-start.3) | collective-permute-done | bytes 106528 | tf_op jit(solution)/shard_map/ppermute | solution.py:513
  48.9 2.7 collective-permute-start.7
  51.7 2.2 collective-permute-done.7.refs_3_
  57.0 3.5 collective-permute-done.5.refs_1_
  60.5 2.4 shard_map.157
  66.5 2.8 broadcast_select_fusion
  69.4 2.6 broadcast_select_fusion.1
  72.1 3.0 broadcast_select_fusion.2
  75.1 3.9 shard_map.158
  83.5 3.6 collective-permute-done.17
  91.1 2.7 collective-permute-done.18.refs_2_
  93.8 2.7 collective-permute-done.20.refs_4_
  97.2 2.4 shard_map.159
  99.6 2.1 collective-permute-start.23
  104.4 6.6 %collective-permute-done.22.refs_2_ = bf16[416,128]{1,0:T(8,128)(2,1)S(1)} collective-permute-done((bf16[416,128]{1,0:T(8,128)(2,1)S(1)}, bf16[416,128]{1,0:T(8,128)(2,1)S(1)}, u32[]{:S(2)}, u32[]{:S(2)}) %collective-permute-start.22) | collective-permute-done | bytes 106528 | tf_op jit(solution)/shard_map/ppermute | solution.py:513
  114.1 2.3 collective-permute-start.24
  120.4 2.4 shard_map.162
  122.8 2.3 collective-permute-start.29
  126.4 3.1 collective-permute-done.29.refs_4_
  129.5 2.4 collective-permute-done.28.refs_3_
  132.2 4.0 %shard_map.163 = (f32[256,768]{1,0:T(8,128)S(1)}, bf16[256,768]{1,0:T(8,128)(2,1)S(1)}, bf16[256,768]{1,0:T(8,128)(2,1)S(1)}, f32[256,768]{1,0:T(8,128)S(1)}, bf...) custom-call(s32[3]{0:T(128)S(1)} %pad_add_fusion.scal, f32[256,768]{1,0:T(8,128)S(1)} %get-tuple-element.98.refs_0_.refs_1_, ...), custom_call_target="tpu_custom_call" | custom-call | bytes 7477248 | tf_op jit(solution)/shard_map/pallas_call | solution.py:124
  137.7 2.2 collective-permute-start.35
  153.3 2.2 shard_map.167
  157.2 2.8 collective-permute-start.41
  172.3 2.3 collective-permute-start.90
  174.6 2.5 collective-permute-start.82
  181.7 4.3 %collective-permute-done.48 = bf16[128,768]{1,0:T(8,128)(2,1)S(1)} collective-permute-done((bf16[128,768]{1,0:T(8,128)(2,1)S(1)}, bf16[128,768]{1,0:T(8,128)(2,1)S(1)}, u32[]{:S(2)}, u32[]{:S(2)}) %collective-permute-start.48) | collective-permute-done | bytes 196640 | tf_op jit(solution)/shard_map/ppermute | solution.py:513
  190.4 2.2 collective-permute-done.49.refs_3_
  192.6 2.3 collective-permute-start.74
  195.0 3.2 shard_map.169
  200.2 3.7 collective-permute-done.52
  205.0 6.5 %collective-permute-done.54 = bf16[128,768]{1,0:T(8,128)(2,1)S(1)} collective-permute-done((bf16[128,768]{1,0:T(8,128)(2,1)S(1)}, bf16[128,768]{1,0:T(8,128)(2,1)S(1)}, u32[]{:S(2)}, u32[]{:S(2)}) %collective-permute-start.54) | collective-permute-done | bytes 196640 | tf_op jit(solution)/shard_map/ppermute | solution.py:513
  214.2 2.2 select_bitcast_fusion.3
  216.5 3.4 fusion.25
  219.9 3.1 fusion.23
  229.2 2.2 shard_map.172
  233.2 2.7 collective-permute-start.57
  237.8 2.5 collective-permute-done.57.refs_2_
  256.8 3.5 collective-permute-done.65
  262.2 3.0 fusion.21
  268.9 4.1 %collective-permute-start.97 = (f32[2,768]{1,0:T(2,128)S(1)}, f32[2,768]{1,0:T(2,128)S(1)}, u32[]{:S(2)}, u32[]{:S(2)}) collective-permute-start(f32[2,768]{1,0:T(2,128)S(1)} %select_add_fusion), channel_id=1, source_target_pairs={{0,12},{4,0},{8,4},{12,8},{1,13},{5,1},{9,5},{13,9},{2,14},{6,2},{... | collective-permute-start | bytes 18440 | tf_op jit(solution)/shard_map/ppermute | solution.py:513
  275.3 2.2 collective-permute-done.96
  285.7 5.7 %collective-permute-start.89 = (bf16[192,768]{0,1:T(8,128)(2,1)S(1)}, bf16[192,768]{0,1:T(8,128)(2,1)S(1)}, u32[]{:S(2)}, u32[]{:S(2)}) collective-permute-start(bf16[192,768]{0,1:T(8,128)(2,1)S(1)} %get-tuple-element.211), channel_id=1, source_target_pairs={{0,12},{4,0},{8,4},{12,8},{1,13},{5,1},{9,5},{13,9},{2,14},{6,2},{... | collective-permute-start | bytes 884744 | tf_op jit(solution)/shard_map/ppermute | solution.py:567
  299.6 9.0 %collective-permute-start.79 = (bf16[192,768]{0,1:T(8,128)(2,1)}, bf16[192,768]{0,1:T(8,128)(2,1)}, u32[]{:S(2)}, u32[]{:S(2)}) collective-permute-start(bf16[192,768]{0,1:T(8,128)(2,1)} %get-tuple-element.216), channel_id=1, source_target_pairs={{0,4},{4,8},{8,12},{12,0},{1,5},{5,9},{9,13},{13,1},{2,6},{6,10},{... | collective-permute-start | bytes 884744 | tf_op jit(solution)/shard_map/ppermute | solution.py:567
  312.4 15.1 %collective-permute-done.88 = bf16[192,768]{0,1:T(8,128)(2,1)S(1)} collective-permute-done((bf16[192,768]{0,1:T(8,128)(2,1)S(1)}, bf16[192,768]{0,1:T(8,128)(2,1)S(1)}, u32[]{:S(2)}, u32[]{:S(2)}) %collective-permute-start.88) | collective-permute-done | bytes 294944 | tf_op jit(solution)/shard_map/ppermute | solution.py:567
  329.4 2.4 fusion.3
  331.8 2.2 copy.61
  338.3 12.1 %collective-permute-done.80 = bf16[192,768]{0,1:T(8,128)(2,1)} collective-permute-done((bf16[192,768]{0,1:T(8,128)(2,1)}, bf16[192,768]{0,1:T(8,128)(2,1)}, u32[]{:S(2)}, u32[]{:S(2)}) %collective-permute-start.80) | collective-permute-done | bytes 294944 | tf_op jit(solution)/shard_map/ppermute | solution.py:567
  350.4 9.2 %collective-permute-start.69 = (f32[256,768]{1,0:T(8,128)}, f32[256,768]{1,0:T(8,128)}, u32[]{:S(2)}, u32[]{:S(2)}) collective-permute-start(f32[256,768]{1,0:T(8,128)} %broadcast_select_fusion.6), channel_id=1, source_target_pairs={{0,16},{16,0},{1,17},{17,1},{2,18},{18,2},{3,19},{19,3},{4,20},{20... | collective-permute-start | bytes 2359304 | tf_op jit(solution)/shard_map/ppermute | solution.py:513
  359.6 3.4 fusion.9
  363.0 2.2 copy.60
  367.2 2.5 collective-permute-start.71
  369.7 5.2 %collective-permute-start.73 = (bf16[192,768]{0,1:T(8,128)(2,1)S(1)}, bf16[192,768]{0,1:T(8,128)(2,1)S(1)}, u32[]{:S(2)}, u32[]{:S(2)}) collective-permute-start(bf16[192,768]{0,1:T(8,128)(2,1)S(1)} %get-tuple-element.223), channel_id=1, source_target_pairs={{0,12},{4,0},{8,4},{12,8},{1,13},{5,1},{9,5},{13,9},{2,14},{6,2},{... | collective-permute-start | bytes 884744 | tf_op jit(solution)/shard_map/ppermute | solution.py:567
  374.9 2.7 collective-permute-start.72
  380.2 2.7 collective-permute-done.73
  382.9 8.4 %collective-permute-done.72 = bf16[192,768]{0,1:T(8,128)(2,1)S(1)} collective-permute-done((bf16[192,768]{0,1:T(8,128)(2,1)S(1)}, bf16[192,768]{0,1:T(8,128)(2,1)S(1)}, u32[]{:S(2)}, u32[]{:S(2)}) %collective-permute-start.72) | collective-permute-done | bytes 294944 | tf_op jit(solution)/shard_map/ppermute | solution.py:567
  (347 shorter events, 151.4 us)
Async XLA Ops:
  0.6 25.9 %collective-permute-start.1 = (bf16[3,768,192]{1,2,0:T(8,128)(2,1)}, bf16[3,768,192]{1,2,0:T(8,128)(2,1)}, u32[]{:S(2)}, u32[]{:S(2)}) collective-permute-start(bf16[3,768,192]{1,2,0:T(8,128)(2,1)} %bitcast.95), channel_id=1, source_target_pairs={{0,16},{16,0},{1,17},{17,1},{2,18},{18,2},{3,19},{19,3},{4,20},{20... | collective-permute-start | bytes 2654216 | tf_op jit(solution)/shard_map/ppermute | solution.py:513
  1.2 15.4 %collective-permute-start.13 = (bf16[192,768]{1,0:T(8,128)(2,1)}, bf16[192,768]{1,0:T(8,128)(2,1)S(1)}, u32[]{:S(2)}, u32[]{:S(2)}) collective-permute-start(bf16[192,768]{1,0:T(8,128)(2,1)} %bitcast.84), channel_id=1, source_target_pairs={{0,3},{1,2},{2,1},{3,0},{4,7},{5,6},{6,5},{7,4},{8,11},{9,10},{10,... | collective-permute-start | bytes 884744 | tf_op jit(solution)/shard_map/ppermute | solution.py:513
  4.7 14.1 %collective-permute-start.12 = (bf16[192,768]{1,0:T(8,128)(2,1)}, bf16[192,768]{1,0:T(8,128)(2,1)S(1)}, u32[]{:S(2)}, u32[]{:S(2)}) collective-permute-start(bf16[192,768]{1,0:T(8,128)(2,1)} %bitcast.85), channel_id=1, source_target_pairs={{0,2},{1,3},{2,0},{3,1},{4,6},{5,7},{6,4},{7,5},{8,10},{9,11},{10,... | collective-permute-start | bytes 884744 | tf_op jit(solution)/shard_map/ppermute | solution.py:513
  5.2 11.1 %collective-permute-start = (bf16[2,768]{1,0:T(2,128)(2,1)}, bf16[2,768]{1,0:T(2,128)(2,1)S(1)}, u32[]{:S(2)}, u32[]{:S(2)}) collective-permute-start(bf16[2,768]{1,0:T(2,128)(2,1)} %bitcast.97), channel_id=1, source_target_pairs={{0,16},{16,0},{1,17},{17,1},{2,18},{18,2},{3,19},{19,3},{4,20},{20... | collective-permute-start | bytes 9224 | tf_op jit(solution)/shard_map/ppermute | solution.py:513
  5.2 59.8 %collective-permute-start.16 = (bf16[768,768]{1,0:T(8,128)(2,1)}, bf16[768,768]{1,0:T(8,128)(2,1)}, u32[]{:S(2)}, u32[]{:S(2)}) collective-permute-start(bf16[768,768]{1,0:T(8,128)(2,1)} %bitcast.93), channel_id=1, source_target_pairs={{0,16},{16,0},{1,17},{17,1},{2,18},{18,2},{3,19},{19,3},{4,20},{20... | collective-permute-start | bytes 3538952 | tf_op jit(solution)/shard_map/ppermute | solution.py:513
  16.3 9.0 %collective-permute-start.11 = (bf16[192,768]{1,0:T(8,128)(2,1)S(1)}, bf16[192,768]{1,0:T(8,128)(2,1)S(1)}, u32[]{:S(2)}, u32[]{:S(2)}) collective-permute-start(bf16[192,768]{1,0:T(8,128)(2,1)S(1)} %bitcast.86), channel_id=1, source_target_pairs={{0,1},{1,0},{2,3},{3,2},{4,5},{5,4},{6,7},{7,6},{8,9},{9,8},{10,11... | collective-permute-start | bytes 884744 | tf_op jit(solution)/shard_map/ppermute | solution.py:513
  16.6 52.8 %collective-permute-start.15 = (bf16[768,768]{1,0:T(8,128)(2,1)}, bf16[768,768]{1,0:T(8,128)(2,1)}, u32[]{:S(2)}, u32[]{:S(2)}) collective-permute-start(bf16[768,768]{1,0:T(8,128)(2,1)} %bitcast.94), channel_id=1, source_target_pairs={{0,16},{16,0},{1,17},{17,1},{2,18},{18,2},{3,19},{19,3},{4,20},{20... | collective-permute-start | bytes 3538952 | tf_op jit(solution)/shard_map/ppermute | solution.py:513
  26.5 45.6 %collective-permute-start.14 = (bf16[4,192,768]{2,1,0:T(8,128)(2,1)}, bf16[4,192,768]{2,1,0:T(8,128)(2,1)}, u32[]{:S(2)}, u32[]{:S(2)}) collective-permute-start(bf16[4,192,768]{2,1,0:T(8,128)(2,1)} %pad_maximum_fusion), channel_id=1, source_target_pairs={{0,16},{16,0},{1,17},{17,1},{2,18},{18,2},{3,19},{19,3},{4,20},{20... | collective-permute-start | bytes 3538952 | tf_op jit(solution)/shard_map/ppermute | solution.py:513
  33.4 7.0 %collective-permute-start.4 = (bf16[416,128]{1,0:T(8,128)(2,1)S(1)}, bf16[416,128]{1,0:T(8,128)(2,1)S(1)}, u32[]{:S(2)}, u32[]{:S(2)}) collective-permute-start(bf16[416,128]{1,0:T(8,128)(2,1)S(1)} %get-tuple-element.87.refs_0_), channel_id=1, source_target_pairs={{0,12},{4,0},{8,4},{12,8},{1,13},{5,1},{9,5},{13,9},{2,14},{6,2},{... | collective-permute-start | bytes 319496 | tf_op jit(solution)/shard_map/ppermute | solution.py:513
  37.0 10.4 %collective-permute-start.3 = (bf16[416,128]{1,0:T(8,128)(2,1)S(1)}, bf16[416,128]{1,0:T(8,128)(2,1)S(1)}, u32[]{:S(2)}, u32[]{:S(2)}) collective-permute-start(bf16[416,128]{1,0:T(8,128)(2,1)S(1)} %get-tuple-element.87.refs_0_), channel_id=1, source_target_pairs={{0,8},{4,12},{8,0},{12,4},{1,9},{5,13},{9,1},{13,5},{2,10},{6,14},... | collective-permute-start | bytes 319496 | tf_op jit(solution)/shard_map/ppermute | solution.py:513
  40.4 7.1 %collective-permute-start.2 = (bf16[416,128]{1,0:T(8,128)(2,1)S(1)}, bf16[416,128]{1,0:T(8,128)(2,1)S(1)}, u32[]{:S(2)}, u32[]{:S(2)}) collective-permute-start(bf16[416,128]{1,0:T(8,128)(2,1)S(1)} %get-tuple-element.87.refs_0_), channel_id=1, source_target_pairs={{0,4},{4,8},{8,12},{12,0},{1,5},{5,9},{9,13},{13,1},{2,6},{6,10},{... | collective-permute-start | bytes 319496 | tf_op jit(solution)/shard_map/ppermute | solution.py:513
  53.8 6.6 %collective-permute-start.5 = (bf16[224,128]{1,0:T(8,128)(2,1)S(1)}, bf16[224,128]{1,0:T(8,128)(2,1)S(1)}, u32[]{:S(2)}, u32[]{:S(2)}) collective-permute-start(bf16[224,128]{1,0:T(8,128)(2,1)S(1)} %get-tuple-element.91.refs_0_), channel_id=1, source_target_pairs={{0,4},{4,8},{8,12},{12,0},{1,5},{5,9},{9,13},{13,1},{2,6},{6,10},{... | collective-permute-start | bytes 172040 | tf_op jit(solution)/shard_map/ppermute | solution.py:513
  62.9 12.1 %collective-permute-start.10 = (bf16[256,192]{1,0:T(8,128)(2,1)S(1)}, bf16[256,192]{1,0:T(8,128)(2,1)S(1)}, u32[]{:S(2)}, u32[]{:S(2)}) collective-permute-start(bf16[256,192]{1,0:T(8,128)(2,1)S(1)} %get-tuple-element.94.refs_1_), channel_id=1, source_target_pairs={{0,3},{1,2},{2,1},{3,0},{4,7},{5,6},{6,5},{7,4},{8,11},{9,10},{10,... | collective-permute-start | bytes 294920 | tf_op jit(solution)/shard_map/ppermute | solution.py:513
  64.5 10.6 %collective-permute-start.9 = (bf16[256,192]{1,0:T(8,128)(2,1)S(1)}, bf16[256,192]{1,0:T(8,128)(2,1)S(1)}, u32[]{:S(2)}, u32[]{:S(2)}) collective-permute-start(bf16[256,192]{1,0:T(8,128)(2,1)S(1)} %get-tuple-element.94.refs_1_), channel_id=1, source_target_pairs={{0,2},{1,3},{2,0},{3,1},{4,6},{5,7},{6,4},{7,5},{8,10},{9,11},{10,... | collective-permute-start | bytes 294920 | tf_op jit(solution)/shard_map/ppermute | solution.py:513
  65.0 10.1 %collective-permute-start.8 = (bf16[256,192]{1,0:T(8,128)(2,1)S(1)}, bf16[256,192]{1,0:T(8,128)(2,1)S(1)}, u32[]{:S(2)}, u32[]{:S(2)}) collective-permute-start(bf16[256,192]{1,0:T(8,128)(2,1)S(1)} %get-tuple-element.94.refs_1_), channel_id=1, source_target_pairs={{0,1},{1,0},{2,3},{3,2},{4,5},{5,4},{6,7},{7,6},{8,9},{9,8},{10,11... | collective-permute-start | bytes 294920 | tf_op jit(solution)/shard_map/ppermute | solution.py:513
  81.9 7.8 %collective-permute-start.19 = (bf16[128,768]{1,0:T(8,128)(2,1)S(1)}, bf16[128,768]{1,0:T(8,128)(2,1)S(1)}, u32[]{:S(2)}, u32[]{:S(2)}) collective-permute-start(bf16[128,768]{1,0:T(8,128)(2,1)S(1)} %get-tuple-element.97), channel_id=1, source_target_pairs={{0,2},{1,3},{2,0},{3,1},{4,6},{5,7},{6,4},{7,5},{8,10},{9,11},{10,... | collective-permute-start | bytes 589832 | tf_op jit(solution)/shard_map/ppermute | solution.py:513
  101.7 9.2 %collective-permute-start.22 = (bf16[416,128]{1,0:T(8,128)(2,1)S(1)}, bf16[416,128]{1,0:T(8,128)(2,1)S(1)}, u32[]{:S(2)}, u32[]{:S(2)}) collective-permute-start(bf16[416,128]{1,0:T(8,128)(2,1)S(1)} %get-tuple-element.99.refs_0_), channel_id=1, source_target_pairs={{0,8},{4,12},{8,0},{12,4},{1,9},{5,13},{9,1},{13,5},{2,10},{6,14},... | collective-permute-start | bytes 319496 | tf_op jit(solution)/shard_map/ppermute | solution.py:513
  101.7 9.2 %collective-permute-start.21 = (bf16[416,128]{1,0:T(8,128)(2,1)S(1)}, bf16[416,128]{1,0:T(8,128)(2,1)S(1)}, u32[]{:S(2)}, u32[]{:S(2)}) collective-permute-start(bf16[416,128]{1,0:T(8,128)(2,1)S(1)} %get-tuple-element.99.refs_0_), channel_id=1, source_target_pairs={{0,4},{4,8},{8,12},{12,0},{1,5},{5,9},{9,13},{13,1},{2,6},{6,10},{... | collective-permute-start | bytes 319496 | tf_op jit(solution)/shard_map/ppermute | solution.py:513
  122.8 6.7 %collective-permute-start.29 = (bf16[256,192]{1,0:T(8,128)(2,1)S(1)}, bf16[256,192]{1,0:T(8,128)(2,1)S(1)}, u32[]{:S(2)}, u32[]{:S(2)}) collective-permute-start(bf16[256,192]{1,0:T(8,128)(2,1)S(1)} %get-tuple-element.105.refs_1_), channel_id=1, source_target_pairs={{0,3},{1,2},{2,1},{3,0},{4,7},{5,6},{6,5},{7,4},{8,11},{9,10},{10,... | collective-permute-start | bytes 294920 | tf_op jit(solution)/shard_map/ppermute | solution.py:513
  125.1 6.8 %collective-permute-start.28 = (bf16[256,192]{1,0:T(8,128)(2,1)S(1)}, bf16[256,192]{1,0:T(8,128)(2,1)S(1)}, u32[]{:S(2)}, u32[]{:S(2)}) collective-permute-start(bf16[256,192]{1,0:T(8,128)(2,1)S(1)} %get-tuple-element.105.refs_1_), channel_id=1, source_target_pairs={{0,2},{1,3},{2,0},{3,1},{4,6},{5,7},{6,4},{7,5},{8,10},{9,11},{10,... | collective-permute-start | bytes 294920 | tf_op jit(solution)/shard_map/ppermute | solution.py:513
  141.2 7.2 %collective-permute-start.32 = (bf16[128,768]{1,0:T(8,128)(2,1)S(1)}, bf16[128,768]{1,0:T(8,128)(2,1)S(1)}, u32[]{:S(2)}, u32[]{:S(2)}) collective-permute-start(bf16[128,768]{1,0:T(8,128)(2,1)S(1)} %get-tuple-element.108), channel_id=1, source_target_pairs={{0,2},{1,3},{2,0},{3,1},{4,6},{5,7},{6,4},{7,5},{8,10},{9,11},{10,... | collective-permute-start | bytes 589832 | tf_op jit(solution)/shard_map/ppermute | solution.py:513
  146.4 13.7 %collective-permute-start.31 = (bf16[128,768]{1,0:T(8,128)(2,1)S(1)}, bf16[128,768]{1,0:T(8,128)(2,1)S(1)}, u32[]{:S(2)}, u32[]{:S(2)}) collective-permute-start(bf16[128,768]{1,0:T(8,128)(2,1)S(1)} %add_convert_fusion.9), channel_id=1, source_target_pairs={{0,2},{1,3},{2,0},{3,1},{4,6},{5,7},{6,4},{7,5},{8,10},{9,11},{10,... | collective-permute-start | bytes 589832 | tf_op jit(solution)/shard_map/ppermute | solution.py:513
  148.5 11.6 %collective-permute-start.33 = (bf16[128,768]{1,0:T(8,128)(2,1)S(1)}, bf16[128,768]{1,0:T(8,128)(2,1)S(1)}, u32[]{:S(2)}, u32[]{:S(2)}) collective-permute-start(bf16[128,768]{1,0:T(8,128)(2,1)S(1)} %add_convert_fusion.8), channel_id=1, source_target_pairs={{0,1},{1,0},{2,3},{3,2},{4,5},{5,4},{6,7},{7,6},{8,9},{9,8},{10,11... | collective-permute-start | bytes 589832 | tf_op jit(solution)/shard_map/ppermute | solution.py:513
  155.6 13.7 %collective-permute-start.47 = (bf16[192,128]{1,0:T(8,128)(2,1)S(1)}, bf16[192,128]{1,0:T(8,128)(2,1)S(1)}, u32[]{:S(2)}, u32[]{:S(2)}) collective-permute-start(bf16[192,128]{1,0:T(8,128)(2,1)S(1)} %get-tuple-element.120.refs_4_), channel_id=1, source_target_pairs={{0,12},{4,0},{8,4},{12,8},{1,13},{5,1},{9,5},{13,9},{2,14},{6,2},{... | collective-permute-start | bytes 147464 | tf_op jit(solution)/shard_map/ppermute | solution.py:513
  156.5 15.8 %collective-permute-start.46 = (bf16[192,128]{1,0:T(8,128)(2,1)S(1)}, bf16[192,128]{1,0:T(8,128)(2,1)S(1)}, u32[]{:S(2)}, u32[]{:S(2)}) collective-permute-start(bf16[192,128]{1,0:T(8,128)(2,1)S(1)} %get-tuple-element.120.refs_4_), channel_id=1, source_target_pairs={{0,8},{4,12},{8,0},{12,4},{1,9},{5,13},{9,1},{13,5},{2,10},{6,14},... | collective-permute-start | bytes 147464 | tf_op jit(solution)/shard_map/ppermute | solution.py:513
  161.9 12.7 %collective-permute-start.45 = (bf16[192,128]{1,0:T(8,128)(2,1)S(1)}, bf16[192,128]{1,0:T(8,128)(2,1)S(1)}, u32[]{:S(2)}, u32[]{:S(2)}) collective-permute-start(bf16[192,128]{1,0:T(8,128)(2,1)S(1)} %get-tuple-element.120.refs_4_), channel_id=1, source_target_pairs={{0,4},{4,8},{8,12},{12,0},{1,5},{5,9},{9,13},{13,1},{2,6},{6,10},{... | collective-permute-start | bytes 147464 | tf_op jit(solution)/shard_map/ppermute | solution.py:513
  168.0 9.1 %collective-permute-start.44 = (bf16[224,128]{1,0:T(8,128)(2,1)S(1)}, bf16[224,128]{1,0:T(8,128)(2,1)S(1)}, u32[]{:S(2)}, u32[]{:S(2)}) collective-permute-start(bf16[224,128]{1,0:T(8,128)(2,1)S(1)} %get-tuple-element.116.refs_0_), channel_id=1, source_target_pairs={{0,12},{4,0},{8,4},{12,8},{1,13},{5,1},{9,5},{13,9},{2,14},{6,2},{... | collective-permute-start | bytes 172040 | tf_op jit(solution)/shard_map/ppermute | solution.py:513
  169.2 8.0 %collective-permute-start.43 = (bf16[224,128]{1,0:T(8,128)(2,1)S(1)}, bf16[224,128]{1,0:T(8,128)(2,1)S(1)}, u32[]{:S(2)}, u32[]{:S(2)}) collective-permute-start(bf16[224,128]{1,0:T(8,128)(2,1)S(1)} %get-tuple-element.116.refs_0_), channel_id=1, source_target_pairs={{0,8},{4,12},{8,0},{12,4},{1,9},{5,13},{9,1},{13,5},{2,10},{6,14},... | collective-permute-start | bytes 172040 | tf_op jit(solution)/shard_map/ppermute | solution.py:513
  169.3 7.9 %collective-permute-start.42 = (bf16[224,128]{1,0:T(8,128)(2,1)S(1)}, bf16[224,128]{1,0:T(8,128)(2,1)S(1)}, u32[]{:S(2)}, u32[]{:S(2)}) collective-permute-start(bf16[224,128]{1,0:T(8,128)(2,1)S(1)} %get-tuple-element.116.refs_0_), channel_id=1, source_target_pairs={{0,4},{4,8},{8,12},{12,0},{1,5},{5,9},{9,13},{13,1},{2,6},{6,10},{... | collective-permute-start | bytes 172040 | tf_op jit(solution)/shard_map/ppermute | solution.py:513
  172.3 44.1 %collective-permute-start.90 = (bf16[768,768]{0,1:T(8,128)(2,1)}, bf16[768,768]{0,1:T(8,128)(2,1)}, u32[]{:S(2)}, u32[]{:S(2)}) collective-permute-start(bf16[768,768]{0,1:T(8,128)(2,1)} %convolution_convert_fusion), channel_id=1, source_target_pairs={{0,16},{1,17},{2,18},{3,19},{4,20},{5,21},{6,22},{7,23},{8,24},{9,... | collective-permute-start | bytes 3538952 | tf_op jit(solution)/shard_map/ppermute | solution.py:550
  174.6 45.2 %collective-permute-start.82 = (bf16[768,768]{0,1:T(8,128)(2,1)S(1)}, bf16[768,768]{0,1:T(8,128)(2,1)}, u32[]{:S(2)}, u32[]{:S(2)}) collective-permute-start(bf16[768,768]{0,1:T(8,128)(2,1)S(1)} %convolution_convert_fusion.2), channel_id=1, source_target_pairs={{0,16},{1,17},{2,18},{3,19},{4,20},{5,21},{6,22},{7,23},{8,24},{9,... | collective-permute-start | bytes 3538952 | tf_op jit(solution)/shard_map/ppermute | solution.py:550
  177.1 35.4 %collective-permute-start.34 = (f32[256,768]{1,0:T(8,128)}, f32[256,768]{1,0:T(8,128)}, u32[]{:S(2)}, u32[]{:S(2)}) collective-permute-start(f32[256,768]{1,0:T(8,128)} %broadcast_select_fusion.8), channel_id=1, source_target_pairs={{0,16},{16,0},{1,17},{17,1},{2,18},{18,2},{3,19},{19,3},{4,20},{20... | collective-permute-start | bytes 2359304 | tf_op jit(solution)/shard_map/ppermute | solution.py:513
  178.7 7.3 %collective-permute-start.48 = (bf16[128,768]{1,0:T(8,128)(2,1)S(1)}, bf16[128,768]{1,0:T(8,128)(2,1)S(1)}, u32[]{:S(2)}, u32[]{:S(2)}) collective-permute-start(bf16[128,768]{1,0:T(8,128)(2,1)S(1)} %get-tuple-element.125), channel_id=1, source_target_pairs={{0,1},{1,0},{2,3},{3,2},{4,5},{5,4},{6,7},{7,6},{8,9},{9,8},{10,11... | collective-permute-start | bytes 589832 | tf_op jit(solution)/shard_map/ppermute | solution.py:513
  179.6 7.4 %collective-permute-start.50 = (bf16[128,768]{1,0:T(8,128)(2,1)S(1)}, bf16[128,768]{1,0:T(8,128)(2,1)S(1)}, u32[]{:S(2)}, u32[]{:S(2)}) collective-permute-start(bf16[128,768]{1,0:T(8,128)(2,1)S(1)} %get-tuple-element.126), channel_id=1, source_target_pairs={{0,2},{1,3},{2,0},{3,1},{4,6},{5,7},{6,4},{7,5},{8,10},{9,11},{10,... | collective-permute-start | bytes 589832 | tf_op jit(solution)/shard_map/ppermute | solution.py:513
  187.1 7.9 %collective-permute-start.51 = (bf16[128,768]{1,0:T(8,128)(2,1)S(1)}, bf16[128,768]{1,0:T(8,128)(2,1)S(1)}, u32[]{:S(2)}, u32[]{:S(2)}) collective-permute-start(bf16[128,768]{1,0:T(8,128)(2,1)S(1)} %add_convert_fusion.4.refs_4_), channel_id=1, source_target_pairs={{0,1},{1,0},{2,3},{3,2},{4,5},{5,4},{6,7},{7,6},{8,9},{9,8},{10,11... | collective-permute-start | bytes 589832 | tf_op jit(solution)/shard_map/ppermute | solution.py:513
  192.6 69.5 %collective-permute-start.74 = (bf16[768,768]{0,1:T(8,128)(2,1)}, bf16[768,768]{0,1:T(8,128)(2,1)}, u32[]{:S(2)}, u32[]{:S(2)}) collective-permute-start(bf16[768,768]{0,1:T(8,128)(2,1)} %pad_maximum_fusion.2), channel_id=1, source_target_pairs={{0,16},{1,17},{2,18},{3,19},{4,20},{5,21},{6,22},{7,23},{8,24},{9,... | collective-permute-start | bytes 3538952 | tf_op jit(solution)/shard_map/ppermute | solution.py:550
  204.0 7.6 %collective-permute-start.54 = (bf16[128,768]{1,0:T(8,128)(2,1)S(1)}, bf16[128,768]{1,0:T(8,128)(2,1)S(1)}, u32[]{:S(2)}, u32[]{:S(2)}) collective-permute-start(bf16[128,768]{1,0:T(8,128)(2,1)S(1)} %get-tuple-element.129), channel_id=1, source_target_pairs={{0,2},{1,3},{2,0},{3,1},{4,6},{5,7},{6,4},{7,5},{8,10},{9,11},{10,... | collective-permute-start | bytes 589832 | tf_op jit(solution)/shard_map/ppermute | solution.py:513
  211.5 12.5 %collective-permute-start.53 = (bf16[128,768]{1,0:T(8,128)(2,1)S(1)}, bf16[128,768]{1,0:T(8,128)(2,1)S(1)}, u32[]{:S(2)}, u32[]{:S(2)}) collective-permute-start(bf16[128,768]{1,0:T(8,128)(2,1)S(1)} %add_convert_fusion.3.refs_0_), channel_id=1, source_target_pairs={{0,2},{1,3},{2,0},{3,1},{4,6},{5,7},{6,4},{7,5},{8,10},{9,11},{10,... | collective-permute-start | bytes 589832 | tf_op jit(solution)/shard_map/ppermute | solution.py:513
  212.5 11.5 %collective-permute-start.55 = (bf16[128,768]{1,0:T(8,128)(2,1)S(1)}, bf16[128,768]{1,0:T(8,128)(2,1)S(1)}, u32[]{:S(2)}, u32[]{:S(2)}) collective-permute-start(bf16[128,768]{1,0:T(8,128)(2,1)S(1)} %add_convert_fusion.2.refs_2_), channel_id=1, source_target_pairs={{0,1},{1,0},{2,3},{3,2},{4,5},{5,4},{6,7},{7,6},{8,9},{9,8},{10,11... | collective-permute-start | bytes 589832 | tf_op jit(solution)/shard_map/ppermute | solution.py:513
  226.1 9.8 %collective-permute-start.58 = (bf16[224,128]{1,0:T(8,128)(2,1)S(1)}, bf16[224,128]{1,0:T(8,128)(2,1)S(1)}, u32[]{:S(2)}, u32[]{:S(2)}) collective-permute-start(bf16[224,128]{1,0:T(8,128)(2,1)S(1)} %get-tuple-element.132.refs_0_), channel_id=1, source_target_pairs={{0,12},{4,0},{8,4},{12,8},{1,13},{5,1},{9,5},{13,9},{2,14},{6,2},{... | collective-permute-start | bytes 172040 | tf_op jit(solution)/shard_map/ppermute | solution.py:513
  231.5 14.6 %collective-permute-start.64 = (bf16[192,128]{1,0:T(8,128)(2,1)S(1)}, bf16[192,128]{1,0:T(8,128)(2,1)S(1)}, u32[]{:S(2)}, u32[]{:S(2)}) collective-permute-start(bf16[192,128]{1,0:T(8,128)(2,1)S(1)} %get-tuple-element.139.refs_4_), channel_id=1, source_target_pairs={{0,12},{4,0},{8,4},{12,8},{1,13},{5,1},{9,5},{13,9},{2,14},{6,2},{... | collective-permute-start | bytes 147464 | tf_op jit(solution)/shard_map/ppermute | solution.py:513
  232.9 13.2 %collective-permute-start.63 = (bf16[192,128]{1,0:T(8,128)(2,1)S(1)}, bf16[192,128]{1,0:T(8,128)(2,1)S(1)}, u32[]{:S(2)}, u32[]{:S(2)}) collective-permute-start(bf16[192,128]{1,0:T(8,128)(2,1)S(1)} %get-tuple-element.139.refs_4_), channel_id=1, source_target_pairs={{0,8},{4,12},{8,0},{12,4},{1,9},{5,13},{9,1},{13,5},{2,10},{6,14},... | collective-permute-start | bytes 147464 | tf_op jit(solution)/shard_map/ppermute | solution.py:513
  233.2 7.1 %collective-permute-start.57 = (bf16[224,128]{1,0:T(8,128)(2,1)S(1)}, bf16[224,128]{1,0:T(8,128)(2,1)S(1)}, u32[]{:S(2)}, u32[]{:S(2)}) collective-permute-start(bf16[224,128]{1,0:T(8,128)(2,1)S(1)} %get-tuple-element.132.refs_0_), channel_id=1, source_target_pairs={{0,8},{4,12},{8,0},{12,4},{1,9},{5,13},{9,1},{13,5},{2,10},{6,14},... | collective-permute-start | bytes 172040 | tf_op jit(solution)/shard_map/ppermute | solution.py:513
  240.3 7.5 %collective-permute-start.62 = (bf16[192,128]{1,0:T(8,128)(2,1)S(1)}, bf16[192,128]{1,0:T(8,128)(2,1)S(1)}, u32[]{:S(2)}, u32[]{:S(2)}) collective-permute-start(bf16[192,128]{1,0:T(8,128)(2,1)S(1)} %get-tuple-element.139.refs_4_), channel_id=1, source_target_pairs={{0,4},{4,8},{8,12},{12,0},{1,5},{5,9},{9,13},{13,1},{2,6},{6,10},{... | collective-permute-start | bytes 147464 | tf_op jit(solution)/shard_map/ppermute | solution.py:513
  247.8 32.5 %collective-permute-start.86 = (bf16[768,768]{0,1:T(8,128)(2,1)S(1)}, bf16[768,768]{0,1:T(8,128)(2,1)S(1)}, u32[]{:S(2)}, u32[]{:S(2)}) collective-permute-start(bf16[768,768]{0,1:T(8,128)(2,1)S(1)} %convolution_convert_fusion.1), channel_id=1, source_target_pairs={{16,0},{17,1},{18,2},{19,3},{20,4},{21,5},{22,6},{23,7},{24,8},{25... | collective-permute-start | bytes 3538952 | tf_op jit(solution)/shard_map/ppermute | solution.py:550
  249.1 42.3 %collective-permute-start.78 = (bf16[768,768]{0,1:T(8,128)(2,1)S(1)}, bf16[768,768]{0,1:T(8,128)(2,1)S(1)}, u32[]{:S(2)}, u32[]{:S(2)}) collective-permute-start(bf16[768,768]{0,1:T(8,128)(2,1)S(1)} %convolution_convert_fusion.3), channel_id=1, source_target_pairs={{16,0},{17,1},{18,2},{19,3},{20,4},{21,5},{22,6},{23,7},{24,8},{25... | collective-permute-start | bytes 3538952 | tf_op jit(solution)/shard_map/ppermute | solution.py:550
  253.6 6.7 %collective-permute-start.65 = (bf16[128,768]{1,0:T(8,128)(2,1)S(1)}, bf16[128,768]{1,0:T(8,128)(2,1)S(1)}, u32[]{:S(2)}, u32[]{:S(2)}) collective-permute-start(bf16[128,768]{1,0:T(8,128)(2,1)S(1)} %get-tuple-element.144), channel_id=1, source_target_pairs={{0,1},{1,0},{2,3},{3,2},{4,5},{5,4},{6,7},{7,6},{8,9},{9,8},{10,11... | collective-permute-start | bytes 589832 | tf_op jit(solution)/shard_map/ppermute | solution.py:513
  274.6 7.1 %collective-permute-start.91 = (bf16[192,768]{0,1:T(8,128)(2,1)}, bf16[192,768]{0,1:T(8,128)(2,1)S(1)}, u32[]{:S(2)}, u32[]{:S(2)}) collective-permute-start(bf16[192,768]{0,1:T(8,128)(2,1)} %get-tuple-element.213), channel_id=1, source_target_pairs={{16,20},{20,24},{24,28},{28,16},{17,21},{21,25},{25,29},{29,17},{1... | collective-permute-start | bytes 884744 | tf_op jit(solution)/shard_map/ppermute | solution.py:567
  281.7 14.7 %collective-permute-start.85 = (bf16[192,768]{0,1:T(8,128)(2,1)S(1)}, bf16[192,768]{0,1:T(8,128)(2,1)S(1)}, u32[]{:S(2)}, u32[]{:S(2)}) collective-permute-start(bf16[192,768]{0,1:T(8,128)(2,1)S(1)} %get-tuple-element.220), channel_id=1, source_target_pairs={{16,28},{20,16},{24,20},{28,24},{17,29},{21,17},{25,21},{29,25},{1... | collective-permute-start | bytes 884744 | tf_op jit(solution)/shard_map/ppermute | solution.py:567
  282.4 82.8 %collective-permute-start.70 = (bf16[768,768]{0,1:T(8,128)(2,1)}, bf16[768,768]{0,1:T(8,128)(2,1)}, u32[]{:S(2)}, u32[]{:S(2)}) collective-permute-start(bf16[768,768]{0,1:T(8,128)(2,1)} %pad_maximum_fusion.1), channel_id=1, source_target_pairs={{16,0},{17,1},{18,2},{19,3},{20,4},{21,5},{22,6},{23,7},{24,8},{25... | collective-permute-start | bytes 3538952 | tf_op jit(solution)/shard_map/ppermute | solution.py:550
  283.7 15.9 %collective-permute-start.87 = (bf16[192,768]{0,1:T(8,128)(2,1)S(1)}, bf16[192,768]{0,1:T(8,128)(2,1)S(1)}, u32[]{:S(2)}, u32[]{:S(2)}) collective-permute-start(bf16[192,768]{0,1:T(8,128)(2,1)S(1)} %get-tuple-element.210), channel_id=1, source_target_pairs={{0,4},{4,8},{8,12},{12,0},{1,5},{5,9},{9,13},{13,1},{2,6},{6,10},{... | collective-permute-start | bytes 884744 | tf_op jit(solution)/shard_map/ppermute | solution.py:567
  285.7 24.8 %collective-permute-start.89 = (bf16[192,768]{0,1:T(8,128)(2,1)S(1)}, bf16[192,768]{0,1:T(8,128)(2,1)S(1)}, u32[]{:S(2)}, u32[]{:S(2)}) collective-permute-start(bf16[192,768]{0,1:T(8,128)(2,1)S(1)} %get-tuple-element.211), channel_id=1, source_target_pairs={{0,12},{4,0},{8,4},{12,8},{1,13},{5,1},{9,5},{13,9},{2,14},{6,2},{... | collective-permute-start | bytes 884744 | tf_op jit(solution)/shard_map/ppermute | solution.py:567
  291.4 36.1 %collective-permute-start.88 = (bf16[192,768]{0,1:T(8,128)(2,1)S(1)}, bf16[192,768]{0,1:T(8,128)(2,1)S(1)}, u32[]{:S(2)}, u32[]{:S(2)}) collective-permute-start(bf16[192,768]{0,1:T(8,128)(2,1)S(1)} %get-tuple-element.212), channel_id=1, source_target_pairs={{0,8},{4,12},{8,0},{12,4},{1,9},{5,13},{9,1},{13,5},{2,10},{6,14},... | collective-permute-start | bytes 884744 | tf_op jit(solution)/shard_map/ppermute | solution.py:567
  297.2 36.8 %collective-permute-start.84 = (bf16[192,768]{0,1:T(8,128)(2,1)}, bf16[192,768]{0,1:T(8,128)(2,1)}, u32[]{:S(2)}, u32[]{:S(2)}) collective-permute-start(bf16[192,768]{0,1:T(8,128)(2,1)} %get-tuple-element.221), channel_id=1, source_target_pairs={{16,24},{20,28},{24,16},{28,20},{17,25},{21,29},{25,17},{29,21},{1... | collective-permute-start | bytes 884744 | tf_op jit(solution)/shard_map/ppermute | solution.py:567
  299.6 35.8 %collective-permute-start.79 = (bf16[192,768]{0,1:T(8,128)(2,1)}, bf16[192,768]{0,1:T(8,128)(2,1)}, u32[]{:S(2)}, u32[]{:S(2)}) collective-permute-start(bf16[192,768]{0,1:T(8,128)(2,1)} %get-tuple-element.216), channel_id=1, source_target_pairs={{0,4},{4,8},{8,12},{12,0},{1,5},{5,9},{9,13},{13,1},{2,6},{6,10},{... | collective-permute-start | bytes 884744 | tf_op jit(solution)/shard_map/ppermute | solution.py:567
  310.5 26.4 %collective-permute-start.81 = (bf16[192,768]{0,1:T(8,128)(2,1)}, bf16[192,768]{0,1:T(8,128)(2,1)}, u32[]{:S(2)}, u32[]{:S(2)}) collective-permute-start(bf16[192,768]{0,1:T(8,128)(2,1)} %get-tuple-element.217), channel_id=1, source_target_pairs={{0,12},{4,0},{8,4},{12,8},{1,13},{5,1},{9,5},{13,9},{2,14},{6,2},{... | collective-permute-start | bytes 884744 | tf_op jit(solution)/shard_map/ppermute | solution.py:567
  327.5 22.9 %collective-permute-start.80 = (bf16[192,768]{0,1:T(8,128)(2,1)}, bf16[192,768]{0,1:T(8,128)(2,1)}, u32[]{:S(2)}, u32[]{:S(2)}) collective-permute-start(bf16[192,768]{0,1:T(8,128)(2,1)} %get-tuple-element.218), channel_id=1, source_target_pairs={{0,8},{4,12},{8,0},{12,4},{1,9},{5,13},{9,1},{13,5},{2,10},{6,14},... | collective-permute-start | bytes 884744 | tf_op jit(solution)/shard_map/ppermute | solution.py:567
  334.0 35.6 %collective-permute-start.75 = (bf16[192,768]{0,1:T(8,128)(2,1)}, bf16[192,768]{0,1:T(8,128)(2,1)}, u32[]{:S(2)}, u32[]{:S(2)}) collective-permute-start(bf16[192,768]{0,1:T(8,128)(2,1)} %get-tuple-element.225), channel_id=1, source_target_pairs={{16,20},{20,24},{24,28},{28,16},{17,21},{21,25},{25,29},{29,17},{1... | collective-permute-start | bytes 884744 | tf_op jit(solution)/shard_map/ppermute | solution.py:567
  335.5 44.7 %collective-permute-start.77 = (bf16[192,768]{0,1:T(8,128)(2,1)}, bf16[192,768]{0,1:T(8,128)(2,1)}, u32[]{:S(2)}, u32[]{:S(2)}) collective-permute-start(bf16[192,768]{0,1:T(8,128)(2,1)} %get-tuple-element.226), channel_id=1, source_target_pairs={{16,28},{20,16},{24,20},{28,24},{17,29},{21,17},{25,21},{29,25},{1... | collective-permute-start | bytes 884744 | tf_op jit(solution)/shard_map/ppermute | solution.py:567
  336.9 43.3 %collective-permute-start.76 = (bf16[192,768]{0,1:T(8,128)(2,1)S(1)}, bf16[192,768]{0,1:T(8,128)(2,1)}, u32[]{:S(2)}, u32[]{:S(2)}) collective-permute-start(bf16[192,768]{0,1:T(8,128)(2,1)S(1)} %get-tuple-element.227), channel_id=1, source_target_pairs={{16,24},{20,28},{24,16},{28,20},{17,25},{21,29},{25,17},{29,21},{1... | collective-permute-start | bytes 884744 | tf_op jit(solution)/shard_map/ppermute | solution.py:567
  350.4 24.5 %collective-permute-start.69 = (f32[256,768]{1,0:T(8,128)}, f32[256,768]{1,0:T(8,128)}, u32[]{:S(2)}, u32[]{:S(2)}) collective-permute-start(f32[256,768]{1,0:T(8,128)} %broadcast_select_fusion.6), channel_id=1, source_target_pairs={{0,16},{16,0},{1,17},{17,1},{2,18},{18,2},{3,19},{19,3},{4,20},{20... | collective-permute-start | bytes 2359304 | tf_op jit(solution)/shard_map/ppermute | solution.py:513
  367.2 13.0 %collective-permute-start.71 = (bf16[192,768]{0,1:T(8,128)(2,1)S(1)}, bf16[192,768]{0,1:T(8,128)(2,1)S(1)}, u32[]{:S(2)}, u32[]{:S(2)}) collective-permute-start(bf16[192,768]{0,1:T(8,128)(2,1)S(1)} %get-tuple-element.222), channel_id=1, source_target_pairs={{0,4},{4,8},{8,12},{12,0},{1,5},{5,9},{9,13},{13,1},{2,6},{6,10},{... | collective-permute-start | bytes 884744 | tf_op jit(solution)/shard_map/ppermute | solution.py:567
  369.7 13.2 %collective-permute-start.73 = (bf16[192,768]{0,1:T(8,128)(2,1)S(1)}, bf16[192,768]{0,1:T(8,128)(2,1)S(1)}, u32[]{:S(2)}, u32[]{:S(2)}) collective-permute-start(bf16[192,768]{0,1:T(8,128)(2,1)S(1)} %get-tuple-element.223), channel_id=1, source_target_pairs={{0,12},{4,0},{8,4},{12,8},{1,13},{5,1},{9,5},{13,9},{2,14},{6,2},{... | collective-permute-start | bytes 884744 | tf_op jit(solution)/shard_map/ppermute | solution.py:567
  374.9 16.4 %collective-permute-start.72 = (bf16[192,768]{0,1:T(8,128)(2,1)S(1)}, bf16[192,768]{0,1:T(8,128)(2,1)S(1)}, u32[]{:S(2)}, u32[]{:S(2)}) collective-permute-start(bf16[192,768]{0,1:T(8,128)(2,1)S(1)} %get-tuple-element.224), channel_id=1, source_target_pairs={{0,8},{4,12},{8,0},{12,4},{1,9},{5,13},{9,1},{13,5},{2,10},{6,14},... | collective-permute-start | bytes 884744 | tf_op jit(solution)/shard_map/ppermute | solution.py:567
  (94 other events, 685.7 us)
